TPU v7x, 32 devices: a whole 2x2x4 slice. The times are simulated.
32 devices in a mesh: dp: 16 (over z, x, core), fsdp: 2 (over y).
Axes of the slice: x: 2, y: 2, z: 4, core: 2. Of those that a mesh axis runs over, the one named last changes fastest.
Arguments:
- adapter_in: bfloat16 [4096, 8192], P(('dp', 'fsdp')), may hold values from -6 to 6
- frozen: bfloat16 [4096, 8192], P(('dp', 'fsdp')), may hold values from -8 to 8
- gain: float32 [8192], replicated, may hold values from 0.25 to 1.75
- adapter_a: bfloat16 [8192, 64], P('fsdp'), may hold values from -0.0625 to 0.0625
- adapter_up_matrix: bfloat16 [64, 8192], P(None, 'fsdp'), may hold values from -0.75 to 0.75
- passages: bfloat16 [128, 8192], P('dp', 'fsdp'), may hold values from -8 to 8
- positive: int32 [128], P('dp'), may hold values from 0 to 127, as said below
Outputs:
- adapter_grads: float32 [2, 64, 8192], P(None, 'fsdp', 'dp')
- loss: float32 [], replicated
Inputs may be any that keep to these rules, and one draw needn't show every extreme that they name: Query i of group g (i from g * 8) has its positive among the passages of the same group, and every passage is the positive of exactly one query.
All inputs are finite; a program needn't handle non-finite values.
Results may differ from a plain program's by a relative error of at most 0.017.
Values may be sent and summed in bfloat16 or wider, within the bound.
A program may use at most 64 MiB of HBM per device.

v0:
```python
import jax
import jax.numpy as jnp
from jax import lax
from jax.sharding import PartitionSpec as P

LEN = 32


adapter_scale_factor = 0.25
inv_temp = 20.0
norm_eps = 1e-05


def contracted_row_product(left, right):
    return lax.dot_general(
        left, right, (((1,), (1,)), ((), ())), preferred_element_type=jnp.float32
    )


def shards(adapter_in, frozen, gain, adapter_a, adapter_up_matrix, passages, positive):
    whole_a, full_up_matrix = (
        lax.all_gather(adapter_a, "fsdp", axis=0, tiled=True),
        lax.all_gather(adapter_up_matrix, "fsdp", axis=1, tiled=True),
    )
    width = whole_a.shape[0]
    queries = adapter_in.shape[0] // LEN
    latent_code = jnp.dot(adapter_in, whole_a, preferred_element_type=jnp.float32).astype(
        jnp.bfloat16
    )
    hidden_state = frozen.astype(jnp.float32) + adapter_scale_factor * jnp.dot(
        latent_code, full_up_matrix, preferred_element_type=jnp.float32
    )
    inv_rms = lax.rsqrt(jnp.mean(hidden_state * hidden_state, axis=-1, keepdims=True) + norm_eps)
    normed = hidden_state * inv_rms * gain
    pooled = jnp.mean(normed.reshape(queries, LEN, width), axis=1)
    length = jnp.sqrt(jnp.sum(pooled * pooled, axis=-1, keepdims=True))
    unit = pooled / length
    query_feat = lax.all_to_all(
        unit.astype(jnp.bfloat16), "fsdp", split_axis=1, concat_axis=0, tiled=True
    )
    pas = passages.astype(jnp.float32)
    squares = lax.psum(jnp.sum(pas * pas, axis=-1), "fsdp")
    passage_unit = (pas / jnp.sqrt(squares)[:, None]).astype(jnp.bfloat16)
    total_pairs = passage_unit.shape[0] * lax.axis_size("dp")
    columns = jnp.arange(total_pairs, dtype=jnp.int32)
    partial_value = contracted_row_product(
        query_feat, lax.all_gather(passage_unit, "dp", axis=0, tiled=True)
    )
    scores = inv_temp * lax.psum_scatter(partial_value, "fsdp", scatter_dimension=0, tiled=True)
    own_pos = lax.dynamic_slice_in_dim(positive, lax.axis_index("fsdp") * queries, queries, 0)
    expo = jnp.exp(scores - inv_temp)
    row_sum = jnp.sum(expo, axis=1)
    onehot = (own_pos[:, None] == columns[None, :]).astype(jnp.float32)
    local_term = jnp.sum(jnp.log(row_sum)) - 2.0 * jnp.sum(scores * onehot)
    col_sum, summed = lax.psum((jnp.sum(expo, axis=0), local_term), ("dp", "fsdp"))
    loss = (summed + jnp.sum(jnp.log(col_sum))) / (2.0 * total_pairs) + inv_temp
    weights = (0.5 * (expo / row_sum[:, None] + expo / col_sum[None, :]) - onehot).astype(
        jnp.bfloat16
    )
    group_weights = lax.all_gather(weights, "fsdp", axis=0, tiled=True)
    grad_feat = jnp.dot(
        group_weights,
        lax.all_gather(passage_unit, "dp", axis=0, tiled=True),
        preferred_element_type=jnp.float32,
    )
    query_grad = lax.all_to_all(
        inv_temp * grad_feat, "fsdp", split_axis=0, concat_axis=1, tiled=True
    )
    pooled_grad = (query_grad - unit * jnp.sum(unit * query_grad, axis=-1, keepdims=True)) / length
    normed_grad = jnp.repeat(pooled_grad / LEN, LEN, axis=0)
    scaled = normed_grad * gain
    hidden_state_gradient = (
        inv_rms * scaled
        - hidden_state * inv_rms**3 * jnp.mean(scaled * hidden_state, axis=-1, keepdims=True)
    ).astype(jnp.bfloat16)
    latent_code_gradient = (
        adapter_scale_factor * contracted_row_product(hidden_state_gradient, full_up_matrix)
    ).astype(jnp.bfloat16)
    grad_a_t = jnp.dot(latent_code_gradient.T, adapter_in, preferred_element_type=jnp.float32)
    up_matrix_gradient = adapter_scale_factor * jnp.dot(
        latent_code.T, hidden_state_gradient, preferred_element_type=jnp.float32
    )
    stacked = jnp.stack([grad_a_t, up_matrix_gradient])
    group_sum = lax.psum_scatter(
        stacked.astype(jnp.bfloat16), "fsdp", scatter_dimension=1, tiled=True
    ).astype(jnp.float32)
    adapter_grads = lax.psum_scatter(group_sum, "dp", scatter_dimension=2, tiled=True)
    return (adapter_grads, loss)


def solution(mesh):
    placed = (
        P(("dp", "fsdp"), None),
        P(("dp", "fsdp"), None),
        P(),
        P("fsdp", None),
        P(None, "fsdp"),
        P("dp", "fsdp"),
        P("dp"),
    )
    return jax.shard_map(
        shards, mesh=mesh, in_specs=placed, out_specs=(P(None, "fsdp", "dp"), P()), check_vma=False
    )
```

profile of v0, /device:TPU:0, one launch (start us, length us, event | category | flops | bytes accessed | tf_op | source)
XLA Modules:
  0.0 275.9 jit_solution(8752264829029274306)
XLA Ops:
  7.2 0.7 all-gather.5.cloned.1.call-update
  8.0 0.7 all-gather.7.cloned.1.call-update
  8.7 1.0 fusion.10
  9.7 5.9 %psum.21 = f32[8]{0:T(128)S(1)} all-reduce(f32[8]{0:T(128)S(1)} %fusion.10), channel_id=1, replica_groups=mesh['dp'=16,'fsdp'=2] {'fsdp'}, use_global_device_ids=true, to_apply=%region_4.0 | all-reduce | flops 8 | bytes 64 | tf_op jit(solution)/shard_map/psum | solution.py:42
  15.6 1.5 fusion.11
  17.1 16.5 %all-gather.5.cloned.1.call-done = bf16[8192,64]{0,1:T(8,128)(2,1)} async-done(((bf16[4096,64]{0,1:T(8,128)(2,1)}), bf16[8192,64]{0,1:T(8,128)(2,1)}) %all-gather.5.cloned.1.call-update) | async-done | bytes 1048592 | tf_op jit(solution)/shard_map/all_gather | solution.py:22
  33.6 2.1 convolution_convert_fusion.1
  35.7 20.8 %all-gather.7.cloned.1.call-done = bf16[64,8192]{1,0:T(8,128)(2,1)} async-done(((bf16[64,4096]{1,0:T(8,128)(2,1)}), bf16[64,8192]{1,0:T(8,128)(2,1)}) %all-gather.7.cloned.1.call-update) | async-done | bytes 1048592 | tf_op jit(solution)/shard_map/all_gather | solution.py:23
  56.5 3.0 %multiply_reduce_fusion = (f32[128]{0:T(128)S(1)}, f32[128,8192]{1,0:T(8,128)S(1)}) fusion(bf16[128,64]{0,1:T(8,128)(2,1)S(1)} %convolution_convert_fusion.1, bf16[64,8192]{1,0:T(8,128)(2,1)} %all-gather.7.cloned.1.call-done, bf16[128,8192]{1,0:T(8,128)(2,1)} %param.8), kind=kOutput, calls=%fused_computation.16 | convolution fusion | flops 139460480 | bytes 7356928 | tf_op jit(solution)/shard_map/dot_general | solution.py:30
  59.5 1.9 copy-done.1
  61.4 0.7 bitcast_reduce_fusion
  62.3 0.7 fusion.21
  63.1 3.3 %all-to-all-start = ((bf16[4,2,4096]{2,0,1:T(4,128)(2,1)}), bf16[4,2,4096]{2,0,1:T(4,128)(2,1)S(1)}, u32[]{:S(2)}, u32[]{:S(2)}) async-start(bf16[4,2,4096]{2,0,1:T(4,128)(2,1)} %fusion.21), calls=%async_computation | async-start | bytes 131072 | tf_op jit(solution)/shard_map/all_to_all | solution.py:38
  67.8 2.7 all-to-all-done
  70.5 26.1 %all-gather.9.cloned.1.call-done = bf16[128,4096]{1,0:T(8,128)(2,1)} async-done(((bf16[8,4096]{1,0:T(8,128)(2,1)}), bf16[128,4096]{1,0:T(8,128)(2,1)}) %all-gather.9.cloned.1.call-update) | async-done | bytes 1048592 | tf_op jit(solution)/shard_map/all_gather | solution.py:47
  96.6 1.6 fusion.22
  98.2 4.9 %all-reduce = f32[8,128]{1,0:T(8,128)S(1)} all-reduce(f32[8,128]{1,0:T(8,128)S(1)} %fusion.22), channel_id=2, replica_groups=mesh['dp'=16,'fsdp'=2] {'fsdp'}, use_global_device_ids=true, to_apply=%region_5.0.clone | all-reduce | flops 1024 | bytes 8192
  103.2 0.7 select_reduce_fusion
  103.8 0.6 log_reduce_fusion.1
  105.7 38.9 %all-reduce.1 = (f32[128]{0:T(128)S(1)}, f32[]{:T(128)}) all-reduce(f32[128]{0:T(128)S(1)} %get-tuple-element.3, f32[]{:T(128)S(6)} %sub.19), channel_id=1, replica_groups=mesh['dp'=16,'fsdp'=2] {'dp','fsdp'}, use_global_device_ids=true, to_apply=%region_8.0 | all-reduce | flops 129 | bytes 1032 | tf_op jit(solution)/shard_map/psum | solution.py:55
  144.7 4.6 %all-gather = bf16[2,4,128]{2,1,0:T(4,128)(2,1)S(1)} all-gather(bf16[1,4,128]{2,1,0:T(4,128)(2,1)S(1)} %fusion.17), channel_id=1, replica_groups=mesh['dp'=16,'fsdp'=2] {'fsdp'}, dimensions={0}, use_global_device_ids=true | all-gather | bytes 3072 | tf_op jit(solution)/shard_map/all_gather | solution.py:60
  149.4 1.5 convolution_multiply_fusion.2
  150.9 7.9 %all_to_all.35 = f32[2,4,4096]{2,1,0:T(4,128)S(1)} all-to-all(f32[2,4,4096]{2,1,0:T(4,128)S(1)} %all_to_all.29), channel_id=1, replica_groups=mesh['dp'=16,'fsdp'=2] {'fsdp'}, dimensions={0} | all-to-all | bytes 262144 | tf_op jit(solution)/shard_map/all_to_all | solution.py:66
  159.1 2.6 fusion.8
  161.7 0.8 fusion.7
  162.6 1.3 copy-done.3
  164.4 4.5 %fusion.2 = bf16[1,64,8192]{2,1,0:T(8,128)(2,1)} fusion(bf16[128,8192]{1,0:T(8,128)(2,1)S(1)} %copy-done, bf16[128,8192]{1,0:T(8,128)(2,1)} %copy-done.3, bf16[64,8192]{1,0:T(8,128)(2,1)} %all-gather.7.cloned.1.call-done), kind=kOutput, calls=%fused_computation.5 | convolution fusion | flops 268976128 | bytes 6291456 | tf_op jit(solution)/shard_map/dot_general | solution.py:79
  168.8 2.8 %pad_maximum_fusion = bf16[2,64,8192]{2,1,0:T(8,128)(2,1)} fusion(bf16[1,64,8192]{2,1,0:T(8,128)(2,1)S(1)} %fusion.3, bf16[1,64,8192]{2,1,0:T(8,128)(2,1)} %fusion.2), kind=kLoop, calls=%fused_computation.17 | loop fusion | flops 1048576 | bytes 4194304 | tf_op jit(solution)/shard_map/stack | solution.py:83
  171.7 30.3 %reduce-scatter.3.cloned.1.call-done = bf16[2,32,8192]{2,1,0:T(8,128)(2,1)} async-done(((bf16[2,64,8192]{2,1,0:T(8,128)(2,1)}), bf16[2,32,8192]{2,1,0:T(8,128)(2,1)}) %reduce-scatter.3.cloned.1.call-update) | async-done | bytes 1048592 | tf_op jit(solution)/shard_map/reduce_scatter | solution.py:84
  202.0 2.7 convert_element_type.41
  204.7 0.6 log_reduce_fusion
  206.6 61.6 %reduce-scatter.5.cloned.1.call-done = f32[2,32,512]{2,1,0:T(8,128)} async-done(((f32[2,32,8192]{2,1,0:T(8,128)}), f32[2,32,512]{2,1,0:T(8,128)}) %reduce-scatter.5.cloned.1.call-update) | async-done | bytes 131088 | tf_op jit(solution)/shard_map/reduce_scatter | solution.py:87
  (33 shorter events, 2.1 us)
Async XLA Ops:
  7.2 26.4 %copy-start = (bf16[128,8192]{1,0:T(8,128)(2,1)S(1)}, bf16[128,8192]{1,0:T(8,128)(2,1)}, u32[]{:S(2)}) copy-start(bf16[128,8192]{1,0:T(8,128)(2,1)} %param.7) | copy-start | bytes 6291460
  7.2 26.4 %all-gather.5.cloned.1.call-start = ((), (), s32[]{:S(2)}) async-start(), calls=%async_computation.4 | async-start | bytes 1572864 | tf_op jit(solution)/shard_map/all_gather | solution.py:22
  7.9 48.6 %all-gather.7.cloned.1.call-start = ((), (), s32[]{:S(2)}) async-start(), calls=%async_computation.5 | async-start | bytes 1572864 | tf_op jit(solution)/shard_map/all_gather | solution.py:23
  8.7 88.0 %all-gather.9.cloned.1.call-start = ((), (), s32[]{:S(2)}) async-start(), calls=%async_computation.6 | async-start | bytes 1114112 | tf_op jit(solution)/shard_map/all_gather | solution.py:47
  35.7 25.7 %copy-start.4 = (f32[8192]{0:T(1024)S(1)}, f32[8192]{0:T(1024)}, u32[]{:S(2)}) copy-start(f32[8192]{0:T(1024)} %param.9) | copy-start | bytes 98308
  59.5 1.9 copy-start.1
  59.5 7.0 %copy-start.6 = (u32[32]{0:T(128)S(1)}, u32[32]{0:T(128)}, u32[]{:S(2)}) copy-start(u32[32]{0:T(128)} %constant.44) | copy-start | bytes 388
  59.5 8.2 %copy-start.5 = (s32[8]{0:T(128)S(1)}, s32[8]{0:T(128)}, u32[]{:S(2)}) copy-start(s32[8]{0:T(128)} %param.13) | copy-start | bytes 100
  63.1 7.4 %all-to-all-start = ((bf16[4,2,4096]{2,0,1:T(4,128)(2,1)}), bf16[4,2,4096]{2,0,1:T(4,128)(2,1)S(1)}, u32[]{:S(2)}, u32[]{:S(2)}) async-start(bf16[4,2,4096]{2,0,1:T(4,128)(2,1)} %fusion.21), calls=%async_computation | async-start | bytes 131072 | tf_op jit(solution)/shard_map/all_to_all | solution.py:38
  66.4 135.6 %reduce-scatter.3.cloned.1.call-start = ((), (), s32[]{:S(2)}) async-start(), calls=%async_computation.7 | async-start | bytes 3145728 | tf_op jit(solution)/shard_map/reduce_scatter | solution.py:84
  150.9 10.8 %copy-start.2 = (f32[128,8192]{1,0:T(8,128)S(1)}, f32[128,8192]{1,0:T(8,128)}, u32[]{:S(2)}) copy-start(f32[128,8192]{1,0:T(8,128)} %copy-done.1) | copy-start | bytes 12582916
  162.6 1.4 copy-start.3
  171.6 96.6 %reduce-scatter.5.cloned.1.call-start = ((), (), s32[]{:S(2)}) async-start(), calls=%async_computation.8 | async-start | bytes 2228224 | tf_op jit(solution)/shard_map/reduce_scatter | solution.py:87
Sparse Core Ops, SparseCore 0:
  9.6 23.9 all-gather.4
  35.1 21.2 all-gather.6
  58.7 37.9 all-gather.8
  171.8 30.1 reduce-scatter.2
  206.6 61.5 reduce-scatter.4
where the time goes:
time: 277 us; the launch traced here: 276 us
  waiting for transfers between devices  159 us (57%)
  blocking collectives  62.2 us (22%)
  between operations  18.3 us (7%)
  other arithmetic  15.4 us (6%)
  matrix products  13 us (5%)
  local copies, waits for them, and re-layouts  4 us (1%)
  starting transfers between devices  3.5 us (1%)
    reduce_scatter x1, waiting for transfers between devices, shards(): lax.psum_scatter(group_sum, 'dp', scatter_dimension=2, tiled=True)  61.6 us
    psum x1, blocking collectives, shards(): lax.psum((jnp.sum(expo, axis=0), local_term), ('dp', 'fsdp'))  38.9 us
    reduce_scatter x1, waiting for transfers between devices, shards(): lax.psum_scatter(stacked.astype(jnp.bfloat16), 'fsdp', scatter_dimension=...  30.3 us
    all_gather x1, waiting for transfers between devices, shards(): lax.all_gather(passage_unit, 'dp', axis=0, tiled=True)  26.1 us
    all_gather x1, waiting for transfers between devices, shards(): lax.all_gather(adapter_up_matrix, 'fsdp', axis=1, tiled=True)  20.8 us
    all_gather x1, waiting for transfers between devices, shards(): lax.all_gather(adapter_a, 'fsdp', axis=0, tiled=True)  16.5 us
    all_to_all x1, blocking collectives, shards(): lax.all_to_all(inv_temp * grad_feat, 'fsdp', split_axis=0, concat_axis=1,...  7.85 us
    psum x1, blocking collectives, shards(): squares = lax.psum(jnp.sum(pas * pas, axis=-1), 'fsdp')  5.86 us
  transfers between devices with their start and end apart: 6, of which 6 were waited for; matrix products, arithmetic and copies ran while one was open for 4% of the time, Pallas kernels for 0%

commit v1 on v0

--- a/solution.py
+++ b/solution.py
@@ -1,6 +1,11 @@
+import functools
+import itertools
+
 import jax
 import jax.numpy as jnp
 from jax import lax
+from jax.experimental import pallas as pl
+from jax.experimental.pallas import tpu as pltpu
 from jax.sharding import PartitionSpec as P
 
 LEN = 32
@@ -88,6 +93,427 @@
     return (adapter_grads, loss)
 
 
+WHOLE = slice(None)
+MESH = pl.DeviceIdType.MESH
+
+
+def fused(
+    bits, sizes,
+    pos_ref, gain_ref, ain_hbm, frz_hbm, a_hbm, up_hbm, pas_hbm,
+    out_ref, loss_ref,
+    ain, frz, a_own, at_oth, at_snd, up, pas, hid, pasm, part,
+    pooled, qg, norms, near, far, rx,
+    lsem, ssem, rsem,
+):
+    tokens, width, rank, queries, rows, chunk = sizes
+    half = width // 2
+    quarter = half // 4
+    dp, fs = lax.axis_index("dp"), lax.axis_index("fsdp")
+    groups = 2 ** bits
+    pairs = groups * rows
+    bit = [(dp // 2 ** b) % 2 for b in range(bits)]
+
+    def peer(mask, flip):
+        there = dp
+        for b in range(bits):
+            if (mask >> b) & 1:
+                there = there + (1 - 2 * bit[b]) * 2 ** b
+        return (there, 1 - fs if flip else fs)
+
+    def remote(src, dst, k, device):
+        return pltpu.make_async_remote_copy(
+            src_ref=src, dst_ref=dst, send_sem=ssem.at[k], recv_sem=rsem.at[k],
+            device_id=device, device_id_type=MESH,
+        )
+
+    started = []
+
+    def send(src, dst, device):
+        copy = remote(src, dst, len(started), device)
+        copy.start()
+        started.append(copy)
+        return copy
+
+    def block(number):
+        return tuple((number // 2 ** b) % 2 for b in reversed(range(bits)))
+
+    own_cols = pl.ds(pl.multiple_of(fs * half, half), half)
+    mine = tuple(reversed(bit))
+    loads = [
+        pltpu.make_async_copy(up_hbm, up.at[:, own_cols], lsem.at[0]),
+        pltpu.make_async_copy(a_hbm, a_own, lsem.at[1]),
+        pltpu.make_async_copy(pas_hbm, pas.at[mine + (WHOLE, own_cols)], lsem.at[2]),
+        pltpu.make_async_copy(ain_hbm, ain, lsem.at[3]),
+        pltpu.make_async_copy(frz_hbm, frz, lsem.at[4]),
+    ]
+    for load in loads:
+        load.start()
+
+    near_masks = [(m, f) for f in (0, 1) for m in range(4) if m or f]
+    far_masks = [4 * m for m in range(1, groups // 4)]
+    barrier = pltpu.get_barrier_semaphore()
+    for m, f in near_masks + [(m, 0) for m in far_masks]:
+        pl.semaphore_signal(barrier, inc=1, device_id=peer(m, f), device_id_type=MESH)
+    pl.semaphore_wait(barrier, len(near_masks) + len(far_masks))
+
+    def q_at(q, base=0):
+        return pl.ds(pl.multiple_of(base + q * quarter, quarter), quarter)
+
+    q0 = dp % 4
+    q2 = q0 + 2 - 4 * bit[1]
+    other = (1 - fs) * half
+
+    def up_at(q, base):
+        return up.at[:, q_at(q, base)]
+
+    def at_at(q):
+        return at_oth.at[:, q_at(q)]
+
+    loads[0].wait()
+    up_y = send(up_at(q0, fs * half), up_at(q0, fs * half), peer(0, 1))
+    loads[1].wait()
+    at_snd[...] = a_own[q_at(q0), :].astype(jnp.float32).T.astype(jnp.bfloat16)
+    at_y = send(at_snd, at_at(q0), peer(0, 1))
+
+    loads[2].wait()
+    upper = list(range(2, bits))
+    orders = (upper + [1, "y", 0], ["y", 1] + upper + [0])
+    strip = half // 2
+    pas_copy = [None, None]
+    pas_step = [0, 0]
+
+    def pas_advance(s):
+        if pas_copy[s] is not None:
+            pas_copy[s].wait_recv()
+        if pas_step[s] == len(orders[s]):
+            return
+        done = orders[s][: pas_step[s]]
+        now = orders[s][pas_step[s]]
+        index = tuple(WHOLE if b in done else bit[b] for b in reversed(range(bits)))
+        if "y" in done:
+            views = [pas.at[index + (WHOLE, pl.ds(h * half + s * strip, strip))] for h in (0, 1)]
+        else:
+            at = pl.multiple_of(fs * half + s * strip, strip)
+            views = [pas.at[index + (WHOLE, pl.ds(at, strip))]]
+        device = peer(0, 1) if now == "y" else peer(2 ** now, 0)
+        pas_copy[s] = Several([send(v, v, device) for v in views])
+        pas_step[s] += 1
+
+    pas_advance(0)
+    pas_advance(1)
+
+    nn = (((1,), (0,)), ((), ()))
+    nt = (((1,), (1,)), ((), ()))
+
+    def mm(left, right, dims):
+        return lax.dot_general(left, right, dims, preferred_element_type=jnp.float32)
+
+    loads[3].wait()
+    latent_own = mm(ain[:, own_cols], a_own[...], nn)
+
+    up_y.wait_recv()
+    up_x = send(up_at(q0, other), up_at(q0, other), peer(2, 0))
+    at_y.wait_recv()
+    at_x = send(at_at(q0), at_at(q0), peer(2, 0))
+    pas_advance(0)
+    pas_advance(1)
+    up_x.wait_recv()
+    up_c = [send(up_at(q, other), up_at(q, other), peer(1, 0)) for q in (q0, q2)]
+    at_x.wait_recv()
+    at_c = [send(at_at(q), at_at(q), peer(1, 0)) for q in (q0, q2)]
+    pas_advance(0)
+    pas_advance(1)
+    for copy in at_c:
+        copy.wait_recv()
+    other_cols = pl.ds(pl.multiple_of(other, half), half)
+    latent = latent_own + mm(ain[:, other_cols], at_oth[...], nt)
+    code = latent.astype(jnp.bfloat16)
+    code_t = code.astype(jnp.float32).T.astype(jnp.bfloat16)
+    for copy in up_c:
+        copy.wait_recv()
+    loads[4].wait()
+
+    chunks = width // chunk
+    lanes = 128
+
+    def cols_of(j):
+        return pl.ds(pl.multiple_of(j * chunk, chunk), chunk)
+
+    def fold(x):
+        total = x[:, :lanes]
+        for at in range(lanes, chunk, lanes):
+            total = total + x[:, at : at + lanes]
+        return total
+
+    def forward(j, total):
+        cols = cols_of(j)
+        value = frz[:, cols].astype(jnp.float32) + adapter_scale_factor * mm(code, up[:, cols], nn)
+        hid[:, cols] = value
+        return total + fold(value * value)
+
+    total = lax.fori_loop(0, chunks, forward, jnp.zeros((tokens, lanes), jnp.float32))
+    inv_rms = lax.rsqrt(jnp.sum(total, axis=1, keepdims=True) / width + norm_eps)
+
+    pas_advance(0)
+    pas_advance(1)
+
+    def of_query(q):
+        return pl.ds(q * LEN, LEN)
+
+    def pool(j, total):
+        cols = cols_of(j)
+        each = [
+            jnp.sum(hid[of_query(q), cols] * inv_rms[q * LEN : (q + 1) * LEN], axis=0, keepdims=True)
+            for q in range(queries)
+        ]
+        value = jnp.concatenate(each, axis=0) * (gain_ref[:, cols] * (1.0 / LEN))
+        pooled[:, cols] = value
+        return total + fold(value * value)
+
+    total = lax.fori_loop(0, chunks, pool, jnp.zeros((queries, lanes), jnp.float32))
+    length = jnp.sqrt(jnp.sum(total, axis=1, keepdims=True))
+    inv_length = 1.0 / length
+
+    while pas_step[0] < len(orders[0]):
+        pas_advance(0)
+        pas_advance(1)
+    pas_advance(0)
+    pas_advance(1)
+
+    def gathered(i, _):
+        pair = [pas[block(2 * i + c)].astype(jnp.float32) for c in (0, 1)]
+        value = jnp.concatenate(pair, axis=0)
+        at = pl.ds(pl.multiple_of(i * 2 * rows, 2 * rows), 2 * rows)
+        pasm[at, :] = value.astype(jnp.bfloat16)
+        square = jnp.sum(value * value, axis=1, keepdims=True)
+        norms[at, :] = jnp.broadcast_to(square, (2 * rows, lanes))
+        return 0
+
+    lax.fori_loop(0, groups // 2, gathered, 0)
+    inv_norm = 1.0 / jnp.sqrt(norms[...].T[0:1, :])
+
+    def score(j, total):
+        cols = cols_of(j)
+        unit = (pooled[:, cols] * inv_length).astype(jnp.bfloat16)
+        return total + mm(unit, pasm[:, cols], nt)
+
+    scores = inv_temp * inv_norm * lax.fori_loop(
+        0, chunks, score, jnp.zeros((queries, pairs), jnp.float32)
+    )
+    expo = jnp.exp(scores - inv_temp)
+    row_sum = jnp.sum(expo, axis=1, keepdims=True)
+    row_at = lax.broadcasted_iota(jnp.int32, (queries, pairs), 0)
+    col_at = lax.broadcasted_iota(jnp.int32, (queries, pairs), 1)
+    onehot = jnp.zeros((queries, pairs), jnp.float32)
+    for q in range(queries):
+        hit = jnp.where(col_at == pos_ref[fs * queries + q], 1.0, 0.0)
+        onehot = onehot + jnp.where(row_at == q, hit, 0.0)
+    term = jnp.log(jnp.broadcast_to(row_sum, (queries, pairs))) * (1.0 / pairs)
+    term = jnp.sum(term - 2.0 * scores * onehot)
+    at8 = lax.broadcasted_iota(jnp.int32, (8, pairs), 0)
+    col_part = jnp.broadcast_to(jnp.sum(expo, axis=0, keepdims=True), (8, pairs))
+    payload = jnp.where(at8 == 0, col_part, jnp.where(at8 == 1, term, 0.0))
+
+    slot = fs * 4 + q0
+    near[slot] = payload
+    copies = [send(near.at[slot], near.at[slot], peer(m, f)) for m, f in near_masks]
+    for copy in copies:
+        copy.wait_recv()
+    summed = near[0]
+    for k in range(1, 8):
+        summed = summed + near[k]
+    slot = dp // 4
+    far[slot] = summed
+    copies = [send(far.at[slot], far.at[slot], peer(m, 0)) for m in far_masks]
+    for copy in copies:
+        copy.wait_recv()
+    summed = far[0]
+    for k in range(1, groups // 4):
+        summed = summed + far[k]
+    col_sum = summed[0:1]
+    loss_ref[0, 0] = (
+        jnp.sum(jnp.log(col_sum) + summed[1:2] * (1.0 / pairs)) / (2.0 * pairs) + inv_temp
+    )
+    weights = 0.5 * (expo / row_sum + expo / col_sum) - onehot
+    weights = weights.astype(jnp.bfloat16).astype(jnp.float32) * (inv_norm * inv_temp)
+    high = weights.astype(jnp.bfloat16).astype(jnp.float32)
+    both = jnp.concatenate([high, weights - high], axis=0).astype(jnp.bfloat16)
+
+    def query_side(j, total):
+        cols = cols_of(j)
+        value = mm(both, pasm[:, cols], nn)
+        value = value[:queries] + value[queries:]
+        qg[:, cols] = value
+        return total + fold(value * (pooled[:, cols] * inv_length))
+
+    total = lax.fori_loop(0, chunks, query_side, jnp.zeros((queries, lanes), jnp.float32))
+    along = jnp.sum(total, axis=1, keepdims=True)
+
+    def scale_side(j, totals):
+        cols = cols_of(j)
+        value = qg[:, cols] - pooled[:, cols] * (inv_length * along)
+        value = value * (inv_length * (1.0 / LEN)) * gain_ref[:, cols]
+        qg[:, cols] = value
+        return tuple(
+            totals[q] + fold(hid[of_query(q), cols] * value[q : q + 1]) for q in range(queries)
+        )
+
+    totals = lax.fori_loop(
+        0, chunks, scale_side, tuple(jnp.zeros((LEN, lanes), jnp.float32) for _ in range(queries))
+    )
+    back = [
+        inv_rms[q * LEN : (q + 1) * LEN] ** 3
+        * (jnp.sum(totals[q], axis=1, keepdims=True) / width)
+        for q in range(queries)
+    ]
+
+    def hidden_side(j, total):
+        cols = cols_of(j)
+        value = jnp.concatenate(
+            [
+                inv_rms[q * LEN : (q + 1) * LEN] * qg[q : q + 1, cols] - hid[of_query(q), cols] * back[q]
+                for q in range(queries)
+            ],
+            axis=0,
+        ).astype(jnp.bfloat16)
+        grad = (adapter_scale_factor * mm(code_t, value, nn)).astype(jnp.bfloat16)
+        for y in (0, 1):
+            part[block(j) + (1, y)] = grad[y * rank // 2 : (y + 1) * rank // 2]
+        return total + mm(value, up[:, cols], nt)
+
+    code_grad = lax.fori_loop(0, chunks, hidden_side, jnp.zeros((tokens, rank), jnp.float32))
+
+    grad_orders = ([0, "y", 1] + upper, [0, 1, "y"] + upper)
+    grad_copy = [None, None]
+    rx_at = [0, len(grad_orders[0])]
+
+    def view(g, done, now, there):
+        index = ()
+        for b in reversed(range(bits)):
+            if b == now:
+                index += (1 - bit[b] if there else bit[b],)
+            else:
+                index += (bit[b] if b in done else WHOLE,)
+        if now == "y":
+            return index + (g, 1 - fs if there else fs)
+        return index + (g, fs if "y" in done else WHOLE)
+
+    def grad_send(g, k):
+        order = grad_orders[g]
+        now = order[k]
+        device = peer(0, 1) if now == "y" else peer(2 ** now, 0)
+        grad_copy[g] = send(part.at[view(g, order[:k], now, True)], rx[rx_at[g] + k], device)
+
+    def grad_add(g, k):
+        order = grad_orders[g]
+        buffer = rx[rx_at[g] + k]
+        kept = view(g, order[:k], order[k], False)
+        grad_copy[g].wait_recv()
+        free = [n for n, i in enumerate(kept) if isinstance(i, slice)]
+        for picks in itertools.product((0, 1), repeat=len(free)):
+            index = list(kept)
+            for n, pick in zip(free, picks):
+                index[n] = pick
+            index = tuple(index)
+            value = part[index].astype(jnp.float32) + buffer[picks].astype(jnp.float32)
+            if k == len(order) - 1:
+                out_ref[g] = value
+            else:
+                part[index] = value.astype(jnp.bfloat16)
+
+    grad_send(1, 0)
+    code_grad_t = (adapter_scale_factor * code_grad).astype(jnp.bfloat16)
+    code_grad_t = code_grad_t.astype(jnp.float32).T.astype(jnp.bfloat16)
+
+    def input_side(j, _):
+        grad = mm(code_grad_t, ain[:, cols_of(j)], nn).astype(jnp.bfloat16)
+        for y in (0, 1):
+            part[block(j) + (0, y)] = grad[y * rank // 2 : (y + 1) * rank // 2]
+        return 0
+
+    lax.fori_loop(0, chunks, input_side, 0)
+    grad_send(0, 0)
+    steps = len(grad_orders[0])
+    for k in range(steps):
+        for g in (1, 0):
+            grad_add(g, k)
+            if k + 1 < steps:
+                grad_send(g, k + 1)
+    for copy in started:
+        copy.wait_send()
+
+
+class Several:
+    def __init__(self, copies):
+        self.copies = copies
+
+    def wait_recv(self):
+        for copy in self.copies:
+            copy.wait_recv()
+
+
+def grad_shapes(bits, rank, chunk, order):
+    shapes = []
+    for k in range(len(order)):
+        gone = order[: k + 1]
+        free = bits - len([b for b in gone if b != "y"]) + (0 if "y" in gone else 1)
+        shapes.append(pltpu.VMEM((2,) * free + (rank // 2, chunk), jnp.bfloat16))
+    return shapes
+
+
+def fused_shards(bits, adapter_in, frozen, gain, adapter_a, adapter_up_matrix, passages, positive):
+    tokens, width = adapter_in.shape
+    rank = adapter_a.shape[1]
+    queries = tokens // LEN
+    rows = passages.shape[0]
+    groups = 2 ** bits
+    chunk = width // groups
+    pairs = groups * rows
+    half = width // 2
+    bf16, f32 = jnp.bfloat16, jnp.float32
+    upper = list(range(2, bits))
+    rx = grad_shapes(bits, rank, chunk, [0, "y", 1] + upper)
+    rx += grad_shapes(bits, rank, chunk, [0, 1, "y"] + upper)
+    copies = 64
+    vmem = pl.BlockSpec(memory_space=pltpu.VMEM)
+    smem = pl.BlockSpec(memory_space=pltpu.SMEM)
+    hbm = pl.BlockSpec(memory_space=pl.ANY)
+    grads, loss = pl.pallas_call(
+        functools.partial(fused, bits, (tokens, width, rank, queries, rows, chunk)),
+        out_shape=(
+            jax.ShapeDtypeStruct((2, rank // 2, chunk), f32),
+            jax.ShapeDtypeStruct((1, 1), f32),
+        ),
+        in_specs=[smem, vmem, hbm, hbm, hbm, hbm, hbm],
+        out_specs=(vmem, smem),
+        scratch_shapes=[
+            pltpu.VMEM((tokens, width), bf16),
+            pltpu.VMEM((tokens, width), bf16),
+            pltpu.VMEM((half, rank), bf16),
+            pltpu.VMEM((rank, half), bf16),
+            pltpu.VMEM((rank, half // 4), bf16),
+            pltpu.VMEM((rank, width), bf16),
+            pltpu.VMEM((2,) * bits + (rows, width), bf16),
+            pltpu.VMEM((tokens, width), f32),
+            pltpu.VMEM((pairs, width), bf16),
+            pltpu.VMEM((2,) * bits + (2, 2, rank // 2, chunk), bf16),
+            pltpu.VMEM((queries, width), f32),
+            pltpu.VMEM((queries, width), f32),
+            pltpu.VMEM((pairs, 128), f32),
+            pltpu.VMEM((8, 8, pairs), f32),
+            pltpu.VMEM((groups // 4, 8, pairs), f32),
+            rx,
+            pltpu.SemaphoreType.DMA((5,)),
+            pltpu.SemaphoreType.DMA((copies,)),
+            pltpu.SemaphoreType.DMA((copies,)),
+        ],
+        compiler_params=pltpu.CompilerParams(
+            collective_id=0, has_side_effects=True, vmem_limit_bytes=56 * 2 ** 20
+        ),
+    )(positive, gain.reshape(1, width), adapter_in, frozen, adapter_a, adapter_up_matrix, passages)
+    return grads, loss.reshape(())
+
+
 def solution(mesh):
     placed = (
         P(("dp", "fsdp"), None),
@@ -98,6 +524,11 @@
         P("dp", "fsdp"),
         P("dp"),
     )
+    groups = mesh.shape["dp"]
+    bits = groups.bit_length() - 1
+    body = shards
+    if mesh.shape["fsdp"] == 2 and 4 < groups <= 16 and groups == 2 ** bits:
+        body = functools.partial(fused_shards, bits)
     return jax.shard_map(
-        shards, mesh=mesh, in_specs=placed, out_specs=(P(None, "fsdp", "dp"), P()), check_vma=False
-    )
+        body, mesh=mesh, in_specs=placed, out_specs=(P(None, "fsdp", "dp"), P()), check_vma=False
+    )

time: 277 us -> 88.5 us (0.32)
  waiting for transfers between devices: 159 us -> 0 us
  Pallas kernels: 0 us -> 81.9 us
  blocking collectives: 62.2 us -> 0 us
  between operations: 18.3 us -> 2.39 us
  other arithmetic: 15.4 us -> 0 us
  matrix products: 13 us -> 0 us
  starting transfers between devices: 3.5 us -> 0 us
    reduce_scatter x2 -> x0, waiting for transfers between devices: 91.9 us -> none  [the longest x1 61.6 us: shards(): lax.psum_scatter(group_sum, 'dp', scatter_dimension=2, tiled=True)]
    pallas_call x0 -> x1, Pallas kernels: none -> 81.9 us  [fused_shards(): pl.pallas_call(functools.partial(fused, bits, (tokens, width, rank, queri...]
    all_gather x3 -> x0, waiting for transfers between devices: 63.4 us -> none  [the longest x1 26.1 us: shards(): lax.all_gather(passage_unit, 'dp', axis=0, tiled=True)]
    psum x2 -> x0, blocking collectives: 44.8 us -> none  [the longest x1 38.9 us: shards(): lax.psum((jnp.sum(expo, axis=0), local_term), ('dp', 'fsdp'))]
    dot_general x6 -> x0, matrix products: 13 us -> none  [the longest x1 4.49 us: shards(): jnp.dot(latent_code_gradient.T, adapter_in, preferred_element_type=jnp.fl...]
    all_to_all x1 -> x0, blocking collectives: 7.85 us -> none  [shards(): lax.all_to_all(inv_temp * grad_feat, 'fsdp', split_axis=0, concat_axis=1,...]
    reduce_sum x8 -> x0, other arithmetic: 6.63 us -> none  [the longest x1 2.58 us: shards(): jnp.mean(scaled * hidden_state, axis=-1, keepdims=True)]
    convert_element_type x4 -> x0, other arithmetic: 5.83 us -> none  [the longest x1 2.71 us: shards(): group_sum = lax.psum_scatter(stacked.astype(jnp.bfloat16), 'fsdp', scatte...]
  transfers between devices with their start and end apart: 6 -> 0, of which waited for: 6 -> 0; matrix products, arithmetic and copies ran while one was open for 4% -> 0% of each run, Pallas kernels for 0% -> 0%
where the time goes in v1:
time: 88.5 us; the launch traced here: 88.2 us
  Pallas kernels  81.9 us (93%)
  local copies, waits for them, and re-layouts  3.94 us (4%)
  between operations  2.39 us (3%)
    pallas_call x1, Pallas kernels, fused_shards(): pl.pallas_call(functools.partial(fused, bits, (tokens, width, rank, queri...  81.9 us
    unnamed x2, local copies, waits for them, and re-layouts  3.94 us

profile of v1, /device:TPU:0, one launch (start us, length us, event | category | flops | bytes accessed | tf_op | source)
XLA Modules:
  0.0 88.2 jit_solution(5252120739246998990)
XLA Ops:
  0.6 2.4 %copy.9.a_hbm = bf16[4096,64]{1,0:T(8,128)(2,1)} copy(bf16[4096,64]{0,1:T(8,128)(2,1)} %param.10) | data formatting | bytes 1048576 | tf_op args[3]
  3.0 81.9 %shard_map.86 = (f32[2,32,512]{2,1,0:T(8,128)}, f32[1,1]{1,0:T(1,128)}) custom-call(s32[8]{0:T(128)} %pos_ref.1, f32[1,8192]{1,0:T(1,128)} %bitcast.2, bf16[128,8192]{1,0:T(8,128)(2,1)} %ain_hbm.1, bf16[128,8192]{1,0:T(8,128)(2,1)} %frz_hbm.1, bf16[4096,64]{1,0:T(8,128)(2,1)} %copy.9.a_hbm, bf16[64,4096]{1,0:T(8,128)(2,1)} %up_hbm.1, bf16[8,4096]{1,0:T(8,128)(2,1)} %pas_hbm.1), custom_call_target="tpu_custom_call" | custom-call | tf_op jit(solution)/shard_map/pallas_call | solution.py:481
  84.9 1.6 %copy.12 = f32[2,32,512]{2,1,0:T(8,128)} copy(f32[2,32,512]{2,1,0:T(8,128)} %get-tuple-element.8) | data formatting | bytes 262144

commit v2 on v1

--- a/solution.py
+++ b/solution.py
@@ -99,10 +99,10 @@
 
 def fused(
     bits, sizes,
-    pos_ref, gain_ref, ain_hbm, frz_hbm, a_hbm, up_hbm, pas_hbm,
+    pos_ref, gain_ref, ain_hbm, frz_hbm, at_hbm, up_hbm, pas_hbm,
     out_ref, loss_ref,
-    ain, frz, a_own, at_oth, at_snd, up, pas, hid, pasm, part,
-    pooled, qg, norms, near, far, rx,
+    ain, frz, at, up, pas, hid, pasm, part,
+    pooled, near, far, rx,
     lsem, ssem, rsem,
 ):
     tokens, width, rank, queries, rows, chunk = sizes
@@ -141,7 +141,7 @@
     mine = tuple(reversed(bit))
     loads = [
         pltpu.make_async_copy(up_hbm, up.at[:, own_cols], lsem.at[0]),
-        pltpu.make_async_copy(a_hbm, a_own, lsem.at[1]),
+        pltpu.make_async_copy(at_hbm, at.at[:, own_cols], lsem.at[1]),
         pltpu.make_async_copy(pas_hbm, pas.at[mine + (WHOLE, own_cols)], lsem.at[2]),
         pltpu.make_async_copy(ain_hbm, ain, lsem.at[3]),
         pltpu.make_async_copy(frz_hbm, frz, lsem.at[4]),
@@ -163,17 +163,14 @@
     q2 = q0 + 2 - 4 * bit[1]
     other = (1 - fs) * half
 
+    def at_at(q, base):
+        return at.at[:, q_at(q, base)]
+
     def up_at(q, base):
         return up.at[:, q_at(q, base)]
 
-    def at_at(q):
-        return at_oth.at[:, q_at(q)]
-
-    loads[0].wait()
-    up_y = send(up_at(q0, fs * half), up_at(q0, fs * half), peer(0, 1))
-    loads[1].wait()
-    at_snd[...] = a_own[q_at(q0), :].astype(jnp.float32).T.astype(jnp.bfloat16)
-    at_y = send(at_snd, at_at(q0), peer(0, 1))
+    at_y = send(at_hbm.at[:, q_at(q0)], at_at(q0, fs * half), peer(0, 1))
+    up_y = send(up_hbm.at[:, q_at(q0)], up_at(q0, fs * half), peer(0, 1))
 
     loads[2].wait()
     upper = list(range(2, bits))
@@ -193,8 +190,8 @@
         if "y" in done:
             views = [pas.at[index + (WHOLE, pl.ds(h * half + s * strip, strip))] for h in (0, 1)]
         else:
-            at = pl.multiple_of(fs * half + s * strip, strip)
-            views = [pas.at[index + (WHOLE, pl.ds(at, strip))]]
+            place = pl.multiple_of(fs * half + s * strip, strip)
+            views = [pas.at[index + (WHOLE, pl.ds(place, strip))]]
         device = peer(0, 1) if now == "y" else peer(2 ** now, 0)
         pas_copy[s] = Several([send(v, v, device) for v in views])
         pas_step[s] += 1
@@ -208,30 +205,32 @@
     def mm(left, right, dims):
         return lax.dot_general(left, right, dims, preferred_element_type=jnp.float32)
 
+    loads[1].wait()
     loads[3].wait()
-    latent_own = mm(ain[:, own_cols], a_own[...], nn)
-
+    latent_own = mm(ain[:, own_cols], at[:, own_cols], nt)
+
+    at_y.wait_recv()
+    at_x = send(at_at(q0, other), at_at(q0, other), peer(2, 0))
     up_y.wait_recv()
     up_x = send(up_at(q0, other), up_at(q0, other), peer(2, 0))
-    at_y.wait_recv()
-    at_x = send(at_at(q0), at_at(q0), peer(2, 0))
     pas_advance(0)
     pas_advance(1)
-    up_x.wait_recv()
-    up_c = [send(up_at(q, other), up_at(q, other), peer(1, 0)) for q in (q0, q2)]
     at_x.wait_recv()
-    at_c = [send(at_at(q), at_at(q), peer(1, 0)) for q in (q0, q2)]
+    at_c = [send(at_at(q, other), at_at(q, other), peer(1, 0)) for q in (q0, q2)]
     pas_advance(0)
-    pas_advance(1)
     for copy in at_c:
         copy.wait_recv()
     other_cols = pl.ds(pl.multiple_of(other, half), half)
-    latent = latent_own + mm(ain[:, other_cols], at_oth[...], nt)
+    latent = latent_own + mm(ain[:, other_cols], at[:, other_cols], nt)
     code = latent.astype(jnp.bfloat16)
     code_t = code.astype(jnp.float32).T.astype(jnp.bfloat16)
+    up_x.wait_recv()
+    up_c = [send(up_at(q, other), up_at(q, other), peer(1, 0)) for q in (q0, q2)]
+    pas_advance(1)
+    loads[0].wait()
+    loads[4].wait()
     for copy in up_c:
         copy.wait_recv()
-    loads[4].wait()
 
     chunks = width // chunk
     lanes = 128
@@ -251,26 +250,29 @@
         hid[:, cols] = value
         return total + fold(value * value)
 
-    total = lax.fori_loop(0, chunks, forward, jnp.zeros((tokens, lanes), jnp.float32))
+    def loop(body, init, unroll=2):
+        return lax.fori_loop(0, chunks, body, init, unroll=unroll)
+
+    def of_query(q):
+        return slice(q * LEN, (q + 1) * LEN)
+
+    total = loop(forward, jnp.zeros((tokens, lanes), jnp.float32))
     inv_rms = lax.rsqrt(jnp.sum(total, axis=1, keepdims=True) / width + norm_eps)
 
     pas_advance(0)
     pas_advance(1)
-
-    def of_query(q):
-        return pl.ds(q * LEN, LEN)
 
     def pool(j, total):
         cols = cols_of(j)
         each = [
-            jnp.sum(hid[of_query(q), cols] * inv_rms[q * LEN : (q + 1) * LEN], axis=0, keepdims=True)
+            jnp.sum(hid[of_query(q), cols] * inv_rms[of_query(q)], axis=0, keepdims=True)
             for q in range(queries)
         ]
         value = jnp.concatenate(each, axis=0) * (gain_ref[:, cols] * (1.0 / LEN))
         pooled[:, cols] = value
         return total + fold(value * value)
 
-    total = lax.fori_loop(0, chunks, pool, jnp.zeros((queries, lanes), jnp.float32))
+    total = loop(pool, jnp.zeros((queries, lanes), jnp.float32))
     length = jnp.sqrt(jnp.sum(total, axis=1, keepdims=True))
     inv_length = 1.0 / length
 
@@ -280,26 +282,30 @@
     pas_advance(0)
     pas_advance(1)
 
-    def gathered(i, _):
-        pair = [pas[block(2 * i + c)].astype(jnp.float32) for c in (0, 1)]
-        value = jnp.concatenate(pair, axis=0)
-        at = pl.ds(pl.multiple_of(i * 2 * rows, 2 * rows), 2 * rows)
-        pasm[at, :] = value.astype(jnp.bfloat16)
-        square = jnp.sum(value * value, axis=1, keepdims=True)
-        norms[at, :] = jnp.broadcast_to(square, (2 * rows, lanes))
-        return 0
-
-    lax.fori_loop(0, groups // 2, gathered, 0)
-    inv_norm = 1.0 / jnp.sqrt(norms[...].T[0:1, :])
-
-    def score(j, total):
+    def meet(j, totals):
+        meets, squares = totals
         cols = cols_of(j)
-        unit = (pooled[:, cols] * inv_length).astype(jnp.bfloat16)
-        return total + mm(unit, pasm[:, cols], nt)
-
-    scores = inv_temp * inv_norm * lax.fori_loop(
-        0, chunks, score, jnp.zeros((queries, pairs), jnp.float32)
-    )
+        value = jnp.concatenate(
+            [pas[block(k) + (WHOLE, cols)].astype(jnp.float32) for k in range(groups)], axis=0
+        )
+        narrow = value.astype(jnp.bfloat16)
+        pasm[:, cols] = narrow
+        gained = (hid[:, cols] * gain_ref[:, cols]).astype(jnp.bfloat16)
+        return meets + mm(gained, narrow, nt), squares + fold(value * value)
+
+    meets, squares = loop(
+        meet, (jnp.zeros((tokens, pairs), jnp.float32), jnp.zeros((pairs, lanes), jnp.float32))
+    )
+    squares = jnp.broadcast_to(jnp.sum(squares, axis=1, keepdims=True), (pairs, lanes))
+    inv_norm = 1.0 / jnp.sqrt(squares.T[0:1, :])
+    met = meets * inv_norm
+    scores = jnp.concatenate(
+        [
+            jnp.sum(met[of_query(q)] * inv_rms[of_query(q)], axis=0, keepdims=True)
+            for q in range(queries)
+        ],
+        axis=0,
+    ) * (inv_length * (inv_temp / LEN))
     expo = jnp.exp(scores - inv_temp)
     row_sum = jnp.sum(expo, axis=1, keepdims=True)
     row_at = lax.broadcasted_iota(jnp.int32, (queries, pairs), 0)
@@ -317,6 +323,20 @@
     slot = fs * 4 + q0
     near[slot] = payload
     copies = [send(near.at[slot], near.at[slot], peer(m, f)) for m, f in near_masks]
+
+    def own_side(j, totals):
+        cols = cols_of(j)
+        value = pooled[:, cols] * gain_ref[:, cols]
+        return tuple(
+            totals[q] + fold(hid[of_query(q), cols] * value[q : q + 1]) for q in range(queries)
+        )
+
+    own = loop(
+        own_side, tuple(jnp.zeros((LEN, lanes), jnp.float32) for _ in range(queries))
+    )
+    own = [
+        jnp.sum(own[q], axis=1, keepdims=True) * inv_length[q : q + 1] for q in range(queries)
+    ]
     for copy in copies:
         copy.wait_recv()
     summed = near[0]
@@ -335,59 +355,48 @@
         jnp.sum(jnp.log(col_sum) + summed[1:2] * (1.0 / pairs)) / (2.0 * pairs) + inv_temp
     )
     weights = 0.5 * (expo / row_sum + expo / col_sum) - onehot
-    weights = weights.astype(jnp.bfloat16).astype(jnp.float32) * (inv_norm * inv_temp)
+    weights = weights.astype(jnp.bfloat16).astype(jnp.float32)
+    along = jnp.sum(weights * scores, axis=1, keepdims=True)
+    shrink = inv_length * (1.0 / LEN)
+    back = []
+    for q in range(queries):
+        across = inv_temp * jnp.sum(met[of_query(q)] * weights[q : q + 1], axis=1, keepdims=True)
+        mean = (across - own[q] * along[q : q + 1]) * shrink[q : q + 1] / width
+        back.append(inv_rms[of_query(q)] ** 3 * mean)
+    weights = weights * (inv_norm * inv_temp)
     high = weights.astype(jnp.bfloat16).astype(jnp.float32)
     both = jnp.concatenate([high, weights - high], axis=0).astype(jnp.bfloat16)
-
-    def query_side(j, total):
-        cols = cols_of(j)
-        value = mm(both, pasm[:, cols], nn)
-        value = value[:queries] + value[queries:]
-        qg[:, cols] = value
-        return total + fold(value * (pooled[:, cols] * inv_length))
-
-    total = lax.fori_loop(0, chunks, query_side, jnp.zeros((queries, lanes), jnp.float32))
-    along = jnp.sum(total, axis=1, keepdims=True)
-
-    def scale_side(j, totals):
-        cols = cols_of(j)
-        value = qg[:, cols] - pooled[:, cols] * (inv_length * along)
-        value = value * (inv_length * (1.0 / LEN)) * gain_ref[:, cols]
-        qg[:, cols] = value
-        return tuple(
-            totals[q] + fold(hid[of_query(q), cols] * value[q : q + 1]) for q in range(queries)
-        )
-
-    totals = lax.fori_loop(
-        0, chunks, scale_side, tuple(jnp.zeros((LEN, lanes), jnp.float32) for _ in range(queries))
-    )
-    back = [
-        inv_rms[q * LEN : (q + 1) * LEN] ** 3
-        * (jnp.sum(totals[q], axis=1, keepdims=True) / width)
-        for q in range(queries)
-    ]
+    inward = inv_length * along
 
     def hidden_side(j, total):
         cols = cols_of(j)
+        two = mm(both, pasm[:, cols], nn)
+        scaled = two[:queries] + two[queries:] - pooled[:, cols] * inward
+        scaled = scaled * shrink * gain_ref[:, cols]
         value = jnp.concatenate(
             [
-                inv_rms[q * LEN : (q + 1) * LEN] * qg[q : q + 1, cols] - hid[of_query(q), cols] * back[q]
+                inv_rms[of_query(q)] * scaled[q : q + 1] - hid[of_query(q), cols] * back[q]
                 for q in range(queries)
             ],
             axis=0,
         ).astype(jnp.bfloat16)
-        grad = (adapter_scale_factor * mm(code_t, value, nn)).astype(jnp.bfloat16)
-        for y in (0, 1):
-            part[block(j) + (1, y)] = grad[y * rank // 2 : (y + 1) * rank // 2]
+        put(1, j, adapter_scale_factor * mm(code_t, value, nn))
         return total + mm(value, up[:, cols], nt)
 
-    code_grad = lax.fori_loop(0, chunks, hidden_side, jnp.zeros((tokens, rank), jnp.float32))
-
-    grad_orders = ([0, "y", 1] + upper, [0, 1, "y"] + upper)
-    grad_copy = [None, None]
-    rx_at = [0, len(grad_orders[0])]
-
-    def view(g, done, now, there):
+    def put(g, j, grad):
+        grad = grad.astype(jnp.bfloat16)
+        for n, (y, h) in enumerate(itertools.product((0, 1), repeat=2)):
+            part[block(j) + (g, y, h)] = grad[n * rank // 4 : (n + 1) * rank // 4]
+
+    code_grad = loop(hidden_side, jnp.zeros((tokens, rank), jnp.float32))
+
+    chains = grad_chains(bits)
+    grad_copy = [None] * len(chains)
+    steps = bits + 1
+
+    def view(n, k, there):
+        g, h, order = chains[n]
+        done, now = order[:k], order[k]
         index = ()
         for b in reversed(range(bits)):
             if b == now:
@@ -395,50 +404,50 @@
             else:
                 index += (bit[b] if b in done else WHOLE,)
         if now == "y":
-            return index + (g, 1 - fs if there else fs)
-        return index + (g, fs if "y" in done else WHOLE)
-
-    def grad_send(g, k):
-        order = grad_orders[g]
-        now = order[k]
+            return index + (g, 1 - fs if there else fs, h)
+        return index + (g, fs if "y" in done else WHOLE, h)
+
+    def grad_send(n, k):
+        now = chains[n][2][k]
         device = peer(0, 1) if now == "y" else peer(2 ** now, 0)
-        grad_copy[g] = send(part.at[view(g, order[:k], now, True)], rx[rx_at[g] + k], device)
-
-    def grad_add(g, k):
-        order = grad_orders[g]
-        buffer = rx[rx_at[g] + k]
-        kept = view(g, order[:k], order[k], False)
-        grad_copy[g].wait_recv()
-        free = [n for n, i in enumerate(kept) if isinstance(i, slice)]
+        grad_copy[n] = send(part.at[view(n, k, True)], rx[n * steps + k], device)
+
+    def grad_add(n, k):
+        g, h, order = chains[n]
+        buffer = rx[n * steps + k]
+        kept = view(n, k, False)
+        grad_copy[n].wait_recv()
+        free = [at for at, i in enumerate(kept) if isinstance(i, slice)]
         for picks in itertools.product((0, 1), repeat=len(free)):
             index = list(kept)
-            for n, pick in zip(free, picks):
-                index[n] = pick
+            for at_dim, pick in zip(free, picks):
+                index[at_dim] = pick
             index = tuple(index)
             value = part[index].astype(jnp.float32) + buffer[picks].astype(jnp.float32)
             if k == len(order) - 1:
-                out_ref[g] = value
+                out_ref[g, h * rank // 4 : (h + 1) * rank // 4] = value
             else:
                 part[index] = value.astype(jnp.bfloat16)
 
-    grad_send(1, 0)
+    early = [n for n, c in enumerate(chains) if c[0] == 1]
+    late = [n for n, c in enumerate(chains) if c[0] == 0]
+    for n in early:
+        grad_send(n, 0)
     code_grad_t = (adapter_scale_factor * code_grad).astype(jnp.bfloat16)
     code_grad_t = code_grad_t.astype(jnp.float32).T.astype(jnp.bfloat16)
 
     def input_side(j, _):
-        grad = mm(code_grad_t, ain[:, cols_of(j)], nn).astype(jnp.bfloat16)
-        for y in (0, 1):
-            part[block(j) + (0, y)] = grad[y * rank // 2 : (y + 1) * rank // 2]
+        put(0, j, mm(code_grad_t, ain[:, cols_of(j)], nn))
         return 0
 
-    lax.fori_loop(0, chunks, input_side, 0)
-    grad_send(0, 0)
-    steps = len(grad_orders[0])
+    loop(input_side, 0)
+    for n in late:
+        grad_send(n, 0)
     for k in range(steps):
-        for g in (1, 0):
-            grad_add(g, k)
+        for n in early + late:
+            grad_add(n, k)
             if k + 1 < steps:
-                grad_send(g, k + 1)
+                grad_send(n, k + 1)
     for copy in started:
         copy.wait_send()
 
@@ -452,12 +461,23 @@
             copy.wait_recv()
 
 
-def grad_shapes(bits, rank, chunk, order):
+def grad_chains(bits):
+    last = list(range(3, bits))
+    return [
+        (1, 0, [0, 1, "y", 2] + last),
+        (1, 1, [0, 2, "y", 1] + last),
+        (0, 0, [0, "y", 1, 2] + last),
+        (0, 1, [0, 2, 1, "y"] + last),
+    ]
+
+
+def grad_shapes(bits, rank, chunk):
     shapes = []
-    for k in range(len(order)):
-        gone = order[: k + 1]
-        free = bits - len([b for b in gone if b != "y"]) + (0 if "y" in gone else 1)
-        shapes.append(pltpu.VMEM((2,) * free + (rank // 2, chunk), jnp.bfloat16))
+    for _, _, order in grad_chains(bits):
+        for k in range(len(order)):
+            gone = order[: k + 1]
+            free = bits - len([b for b in gone if b != "y"]) + (0 if "y" in gone else 1)
+            shapes.append(pltpu.VMEM((2,) * free + (rank // 4, chunk), jnp.bfloat16))
     return shapes
 
 
@@ -471,9 +491,7 @@
     pairs = groups * rows
     half = width // 2
     bf16, f32 = jnp.bfloat16, jnp.float32
-    upper = list(range(2, bits))
-    rx = grad_shapes(bits, rank, chunk, [0, "y", 1] + upper)
-    rx += grad_shapes(bits, rank, chunk, [0, 1, "y"] + upper)
+    rx = grad_shapes(bits, rank, chunk)
     copies = 64
     vmem = pl.BlockSpec(memory_space=pltpu.VMEM)
     smem = pl.BlockSpec(memory_space=pltpu.SMEM)
@@ -489,17 +507,13 @@
         scratch_shapes=[
             pltpu.VMEM((tokens, width), bf16),
             pltpu.VMEM((tokens, width), bf16),
-            pltpu.VMEM((half, rank), bf16),
-            pltpu.VMEM((rank, half), bf16),
-            pltpu.VMEM((rank, half // 4), bf16),
+            pltpu.VMEM((rank, width), bf16),
             pltpu.VMEM((rank, width), bf16),
             pltpu.VMEM((2,) * bits + (rows, width), bf16),
             pltpu.VMEM((tokens, width), f32),
             pltpu.VMEM((pairs, width), bf16),
-            pltpu.VMEM((2,) * bits + (2, 2, rank // 2, chunk), bf16),
+            pltpu.VMEM((2,) * bits + (2, 2, 2, rank // 4, chunk), bf16),
             pltpu.VMEM((queries, width), f32),
-            pltpu.VMEM((queries, width), f32),
-            pltpu.VMEM((pairs, 128), f32),
             pltpu.VMEM((8, 8, pairs), f32),
             pltpu.VMEM((groups // 4, 8, pairs), f32),
             rx,
@@ -510,7 +524,7 @@
         compiler_params=pltpu.CompilerParams(
             collective_id=0, has_side_effects=True, vmem_limit_bytes=56 * 2 ** 20
         ),
-    )(positive, gain.reshape(1, width), adapter_in, frozen, adapter_a, adapter_up_matrix, passages)
+    )(positive, gain.reshape(1, width), adapter_in, frozen, adapter_a.T, adapter_up_matrix, passages)
     return grads, loss.reshape(())
 
 

time: 88.5 us -> 77 us (0.87)
  Pallas kernels: 81.9 us -> 72.8 us
  local copies, waits for them, and re-layouts: 3.94 us -> 1.57 us
    pallas_call x1, Pallas kernels: 81.9 us -> 72.8 us  [fused_shards(): pl.pallas_call(functools.partial(fused, bits, (tokens, width, rank, queri...]
    unnamed x2 -> x1, local copies, waits for them, and re-layouts: 3.94 us -> 1.57 us
where the time goes in v2:
time: 77 us; the launch traced here: 76.8 us
  Pallas kernels  72.8 us (95%)
  between operations  2.45 us (3%)
  local copies, waits for them, and re-layouts  1.57 us (2%)
    pallas_call x1, Pallas kernels, fused_shards(): pl.pallas_call(functools.partial(fused, bits, (tokens, width, rank, queri...  72.8 us
    unnamed x1, local copies, waits for them, and re-layouts  1.57 us

profile of v2, /device:TPU:0, one launch (start us, length us, event | category | flops | bytes accessed | tf_op | source)
XLA Modules:
  0.0 76.8 jit_solution(11422636450308669586)
XLA Ops:
  0.6 72.8 %shard_map.86 = (f32[2,32,512]{2,1,0:T(8,128)}, f32[1,1]{1,0:T(1,128)}) custom-call(s32[8]{0:T(128)} %pos_ref.1, f32[1,8192]{1,0:T(1,128)} %bitcast.4, bf16[128,8192]{1,0:T(8,128)(2,1)} %ain_hbm.1, bf16[128,8192]{1,0:T(8,128)(2,1)} %frz_hbm.1, bf16[64,4096]{1,0:T(8,128)(2,1)} %bitcast.3, bf16[64,4096]{1,0:T(8,128)(2,1)} %up_hbm.1, bf16[8,4096]{1,0:T(8,128)(2,1)} %pas_hbm.1), custom_call_target="tpu_custom_call" | custom-call | tf_op jit(solution)/shard_map/pallas_call | solution.py:499
  73.4 1.6 %copy.11 = f32[2,32,512]{2,1,0:T(8,128)} copy(f32[2,32,512]{2,1,0:T(8,128)} %get-tuple-element.8) | data formatting | bytes 262144

commit v3 on v2

--- a/solution.py
+++ b/solution.py
@@ -169,35 +169,48 @@
     def up_at(q, base):
         return up.at[:, q_at(q, base)]
 
+    far_first = list(range(2, bits))[::-1]
+    orders = (
+        ["y", 1] + far_first + [0],
+        [1, "y"] + far_first + [0],
+        far_first + [1, "y", 0],
+        far_first + ["y", 1, 0],
+    )
+    strips = len(orders)
+    strip = half // strips
+    pas_copy = [None] * strips
+    pas_step = [0] * strips
+
+    def pas_advance(*which):
+        for s in which:
+            if pas_copy[s] is not None:
+                for copy in pas_copy[s]:
+                    copy.wait_recv()
+            done = orders[s][: pas_step[s]]
+            pas_step[s] += 1
+            if len(done) == len(orders[s]):
+                continue
+            now = orders[s][len(done)]
+            index = tuple(WHOLE if b in done else bit[b] for b in reversed(range(bits)))
+            device = peer(0, 1) if now == "y" else peer(2 ** now, 0)
+            place = pl.multiple_of(fs * half + s * strip, strip)
+            if not done:
+                source = pas_hbm.at[:, s * strip : (s + 1) * strip]
+                target = pas.at[index + (WHOLE, pl.ds(place, strip))]
+                pas_copy[s] = [send(source, target, device)]
+                continue
+            places = [place]
+            if "y" in done:
+                places = [h * half + s * strip for h in (0, 1)]
+            views = [pas.at[index + (WHOLE, pl.ds(p, strip))] for p in places]
+            pas_copy[s] = [send(v, v, device) for v in views]
+
+    pas_advance(0, 1, 2, 3)
     at_y = send(at_hbm.at[:, q_at(q0)], at_at(q0, fs * half), peer(0, 1))
     up_y = send(up_hbm.at[:, q_at(q0)], up_at(q0, fs * half), peer(0, 1))
 
     loads[2].wait()
-    upper = list(range(2, bits))
-    orders = (upper + [1, "y", 0], ["y", 1] + upper + [0])
-    strip = half // 2
-    pas_copy = [None, None]
-    pas_step = [0, 0]
-
-    def pas_advance(s):
-        if pas_copy[s] is not None:
-            pas_copy[s].wait_recv()
-        if pas_step[s] == len(orders[s]):
-            return
-        done = orders[s][: pas_step[s]]
-        now = orders[s][pas_step[s]]
-        index = tuple(WHOLE if b in done else bit[b] for b in reversed(range(bits)))
-        if "y" in done:
-            views = [pas.at[index + (WHOLE, pl.ds(h * half + s * strip, strip))] for h in (0, 1)]
-        else:
-            place = pl.multiple_of(fs * half + s * strip, strip)
-            views = [pas.at[index + (WHOLE, pl.ds(place, strip))]]
-        device = peer(0, 1) if now == "y" else peer(2 ** now, 0)
-        pas_copy[s] = Several([send(v, v, device) for v in views])
-        pas_step[s] += 1
-
-    pas_advance(0)
-    pas_advance(1)
+    pas_advance(0, 1, 2, 3)
 
     nn = (((1,), (0,)), ((), ()))
     nt = (((1,), (1,)), ((), ()))
@@ -213,11 +226,9 @@
     at_x = send(at_at(q0, other), at_at(q0, other), peer(2, 0))
     up_y.wait_recv()
     up_x = send(up_at(q0, other), up_at(q0, other), peer(2, 0))
-    pas_advance(0)
-    pas_advance(1)
+    pas_advance(0, 1, 2, 3)
     at_x.wait_recv()
     at_c = [send(at_at(q, other), at_at(q, other), peer(1, 0)) for q in (q0, q2)]
-    pas_advance(0)
     for copy in at_c:
         copy.wait_recv()
     other_cols = pl.ds(pl.multiple_of(other, half), half)
@@ -226,7 +237,8 @@
     code_t = code.astype(jnp.float32).T.astype(jnp.bfloat16)
     up_x.wait_recv()
     up_c = [send(up_at(q, other), up_at(q, other), peer(1, 0)) for q in (q0, q2)]
-    pas_advance(1)
+    for _ in range(bits - 3):
+        pas_advance(0, 1, 2, 3)
     loads[0].wait()
     loads[4].wait()
     for copy in up_c:
@@ -236,6 +248,8 @@
     lanes = 128
 
     def cols_of(j):
+        if isinstance(j, int):
+            return slice(j * chunk, (j + 1) * chunk)
         return pl.ds(pl.multiple_of(j * chunk, chunk), chunk)
 
     def fold(x):
@@ -259,8 +273,7 @@
     total = loop(forward, jnp.zeros((tokens, lanes), jnp.float32))
     inv_rms = lax.rsqrt(jnp.sum(total, axis=1, keepdims=True) / width + norm_eps)
 
-    pas_advance(0)
-    pas_advance(1)
+    pas_advance(0, 1, 2, 3)
 
     def pool(j, total):
         cols = cols_of(j)
@@ -275,12 +288,6 @@
     total = loop(pool, jnp.zeros((queries, lanes), jnp.float32))
     length = jnp.sqrt(jnp.sum(total, axis=1, keepdims=True))
     inv_length = 1.0 / length
-
-    while pas_step[0] < len(orders[0]):
-        pas_advance(0)
-        pas_advance(1)
-    pas_advance(0)
-    pas_advance(1)
 
     def meet(j, totals):
         meets, squares = totals
@@ -293,9 +300,12 @@
         gained = (hid[:, cols] * gain_ref[:, cols]).astype(jnp.bfloat16)
         return meets + mm(gained, narrow, nt), squares + fold(value * value)
 
-    meets, squares = loop(
-        meet, (jnp.zeros((tokens, pairs), jnp.float32), jnp.zeros((pairs, lanes), jnp.float32))
-    )
+    totals = jnp.zeros((tokens, pairs), jnp.float32), jnp.zeros((pairs, lanes), jnp.float32)
+    for s in range(strips):
+        pas_advance(s)
+        for h, n in itertools.product((0, 1), range(strip // chunk)):
+            totals = meet((h * half + s * strip) // chunk + n, totals)
+    meets, squares = totals
     squares = jnp.broadcast_to(jnp.sum(squares, axis=1, keepdims=True), (pairs, lanes))
     inv_norm = 1.0 / jnp.sqrt(squares.T[0:1, :])
     met = meets * inv_norm
@@ -388,7 +398,14 @@
         for n, (y, h) in enumerate(itertools.product((0, 1), repeat=2)):
             part[block(j) + (g, y, h)] = grad[n * rank // 4 : (n + 1) * rank // 4]
 
-    code_grad = loop(hidden_side, jnp.zeros((tokens, rank), jnp.float32))
+    def sided(body, side, init):
+        def of(i, carry):
+            return body(2 * i + side, carry)
+
+        return lax.fori_loop(0, chunks // 2, of, init, unroll=2)
+
+    theirs, ours = 1 - bit[0], bit[0]
+    code_grad = sided(hidden_side, theirs, jnp.zeros((tokens, rank), jnp.float32))
 
     chains = grad_chains(bits)
     grad_copy = [None] * len(chains)
@@ -433,6 +450,7 @@
     late = [n for n, c in enumerate(chains) if c[0] == 0]
     for n in early:
         grad_send(n, 0)
+    code_grad = sided(hidden_side, ours, code_grad)
     code_grad_t = (adapter_scale_factor * code_grad).astype(jnp.bfloat16)
     code_grad_t = code_grad_t.astype(jnp.float32).T.astype(jnp.bfloat16)
 
@@ -440,9 +458,10 @@
         put(0, j, mm(code_grad_t, ain[:, cols_of(j)], nn))
         return 0
 
-    loop(input_side, 0)
+    sided(input_side, theirs, 0)
     for n in late:
         grad_send(n, 0)
+    sided(input_side, ours, 0)
     for k in range(steps):
         for n in early + late:
             grad_add(n, k)
@@ -450,15 +469,6 @@
                 grad_send(n, k + 1)
     for copy in started:
         copy.wait_send()
-
-
-class Several:
-    def __init__(self, copies):
-        self.copies = copies
-
-    def wait_recv(self):
-        for copy in self.copies:
-            copy.wait_recv()
 
 
 def grad_chains(bits):
@@ -492,7 +502,7 @@
     half = width // 2
     bf16, f32 = jnp.bfloat16, jnp.float32
     rx = grad_shapes(bits, rank, chunk)
-    copies = 64
+    copies = 80
     vmem = pl.BlockSpec(memory_space=pltpu.VMEM)
     smem = pl.BlockSpec(memory_space=pltpu.SMEM)
     hbm = pl.BlockSpec(memory_space=pl.ANY)
@@ -541,7 +551,7 @@
     groups = mesh.shape["dp"]
     bits = groups.bit_length() - 1
     body = shards
-    if mesh.shape["fsdp"] == 2 and 4 < groups <= 16 and groups == 2 ** bits:
+    if mesh.shape["fsdp"] == 2 and 8 <= groups <= 16 and groups == 2 ** bits:
         body = functools.partial(fused_shards, bits)
     return jax.shard_map(
         body, mesh=mesh, in_specs=placed, out_specs=(P(None, "fsdp", "dp"), P()), check_vma=False

time: 77 us -> 65.6 us (0.85)
  Pallas kernels: 72.8 us -> 61.4 us
    pallas_call x1, Pallas kernels: 72.8 us -> 61.4 us  [fused_shards(): pl.pallas_call(functools.partial(fused, bits, (tokens, width, rank, queri...]
where the time goes in v3:
time: 65.6 us; the launch traced here: 65.4 us
  Pallas kernels  61.4 us (94%)
  between operations  2.45 us (4%)
  local copies, waits for them, and re-layouts  1.57 us (2%)
    pallas_call x1, Pallas kernels, fused_shards(): pl.pallas_call(functools.partial(fused, bits, (tokens, width, rank, queri...  61.4 us
    unnamed x1, local copies, waits for them, and re-layouts  1.57 us

profile of v3, /device:TPU:0, one launch (start us, length us, event | category | flops | bytes accessed | tf_op | source)
XLA Modules:
  0.0 65.4 jit_solution(18343322771360558982)
XLA Ops:
  0.6 61.4 %shard_map.86 = (f32[2,32,512]{2,1,0:T(8,128)}, f32[1,1]{1,0:T(1,128)}) custom-call(s32[8]{0:T(128)} %pos_ref.1, f32[1,8192]{1,0:T(1,128)} %bitcast.4, bf16[128,8192]{1,0:T(8,128)(2,1)} %ain_hbm.1, bf16[128,8192]{1,0:T(8,128)(2,1)} %frz_hbm.1, bf16[64,4096]{1,0:T(8,128)(2,1)} %bitcast.3, bf16[64,4096]{1,0:T(8,128)(2,1)} %up_hbm.1, bf16[8,4096]{1,0:T(8,128)(2,1)} %pas_hbm.1), custom_call_target="tpu_custom_call" | custom-call | tf_op jit(solution)/shard_map/pallas_call | solution.py:509
  62.0 1.6 %copy.11 = f32[2,32,512]{2,1,0:T(8,128)} copy(f32[2,32,512]{2,1,0:T(8,128)} %get-tuple-element.8) | data formatting | bytes 262144

commit v4 on v3

--- a/solution.py
+++ b/solution.py
@@ -102,7 +102,7 @@
     pos_ref, gain_ref, ain_hbm, frz_hbm, at_hbm, up_hbm, pas_hbm,
     out_ref, loss_ref,
     ain, frz, at, up, pas, hid, pasm, part,
-    pooled, near, far, rx,
+    pooled, scaled, near, far, rx,
     lsem, ssem, rsem,
 ):
     tokens, width, rank, queries, rows, chunk = sizes
@@ -156,18 +156,28 @@
         pl.semaphore_signal(barrier, inc=1, device_id=peer(m, f), device_id_type=MESH)
     pl.semaphore_wait(barrier, len(near_masks) + len(far_masks))
 
-    def q_at(q, base=0):
-        return pl.ds(pl.multiple_of(base + q * quarter, quarter), quarter)
+    def q_at(q, base=0, piece=None):
+        if piece is None:
+            return pl.ds(pl.multiple_of(base + q * quarter, quarter), quarter)
+        size = quarter // 2
+        return pl.ds(pl.multiple_of(base + q * quarter + piece * size, size), size)
 
     q0 = dp % 4
+    q1 = q0 + 1 - 2 * bit[0]
     q2 = q0 + 2 - 4 * bit[1]
+    q3 = q1 + 2 - 4 * bit[1]
     other = (1 - fs) * half
-
-    def at_at(q, base):
-        return at.at[:, q_at(q, base)]
-
-    def up_at(q, base):
-        return up.at[:, q_at(q, base)]
+    pieces = (0, 1)
+
+    def across(whole, own):
+        return [
+            send(own.at[:, q_at(q0, 0, i)], whole.at[:, q_at(q0, fs * half, i)], peer(0, 1))
+            for i in pieces
+        ]
+
+    def pass_on(whole, q, i, mask):
+        view = whole.at[:, q_at(q, other, i)]
+        return send(view, view, peer(mask, 0))
 
     far_first = list(range(2, bits))[::-1]
     orders = (
@@ -206,8 +216,8 @@
             pas_copy[s] = [send(v, v, device) for v in views]
 
     pas_advance(0, 1, 2, 3)
-    at_y = send(at_hbm.at[:, q_at(q0)], at_at(q0, fs * half), peer(0, 1))
-    up_y = send(up_hbm.at[:, q_at(q0)], up_at(q0, fs * half), peer(0, 1))
+    at_y = across(at, at_hbm)
+    up_y = across(up, up_hbm)
 
     loads[2].wait()
     pas_advance(0, 1, 2, 3)
@@ -220,29 +230,37 @@
 
     loads[1].wait()
     loads[3].wait()
-    latent_own = mm(ain[:, own_cols], at[:, own_cols], nt)
-
-    at_y.wait_recv()
-    at_x = send(at_at(q0, other), at_at(q0, other), peer(2, 0))
-    up_y.wait_recv()
-    up_x = send(up_at(q0, other), up_at(q0, other), peer(2, 0))
+    latent = mm(ain[:, own_cols], at[:, own_cols], nt)
+
+    def quarter_of(q):
+        cols = q_at(q, other)
+        return mm(ain[:, cols], at[:, cols], nt)
+
+    at_x, at_c, up_x, up_c = [], [], [], []
+    for i in pieces:
+        at_y[i].wait_recv()
+        at_x.append(pass_on(at, q0, i, 2))
+        at_c.append(pass_on(at, q0, i, 1))
+    for i in pieces:
+        up_y[i].wait_recv()
+        up_x.append(pass_on(up, q0, i, 2))
+        up_c.append(pass_on(up, q0, i, 1))
     pas_advance(0, 1, 2, 3)
-    at_x.wait_recv()
-    at_c = [send(at_at(q, other), at_at(q, other), peer(1, 0)) for q in (q0, q2)]
-    for copy in at_c:
+    latent = latent + quarter_of(q0)
+    for i in pieces:
+        at_x[i].wait_recv()
+        at_c.append(pass_on(at, q2, i, 1))
+    latent = latent + quarter_of(q2)
+    for copy in at_c[:2]:
         copy.wait_recv()
-    other_cols = pl.ds(pl.multiple_of(other, half), half)
-    latent = latent_own + mm(ain[:, other_cols], at[:, other_cols], nt)
+    latent = latent + quarter_of(q1)
+    for copy in at_c[2:]:
+        copy.wait_recv()
+    latent = latent + quarter_of(q3)
     code = latent.astype(jnp.bfloat16)
     code_t = code.astype(jnp.float32).T.astype(jnp.bfloat16)
-    up_x.wait_recv()
-    up_c = [send(up_at(q, other), up_at(q, other), peer(1, 0)) for q in (q0, q2)]
-    for _ in range(bits - 3):
-        pas_advance(0, 1, 2, 3)
     loads[0].wait()
     loads[4].wait()
-    for copy in up_c:
-        copy.wait_recv()
 
     chunks = width // chunk
     lanes = 128
@@ -270,7 +288,21 @@
     def of_query(q):
         return slice(q * LEN, (q + 1) * LEN)
 
-    total = loop(forward, jnp.zeros((tokens, lanes), jnp.float32))
+    def forward_part(start, count, total):
+        return lax.fori_loop(0, count, lambda j, t: forward(start + j, t), total, unroll=2)
+
+    part_size = chunks // 4
+    total = jnp.zeros((tokens, lanes), jnp.float32)
+    total = forward_part(fs * (chunks // 2), part_size, total)
+    for i in pieces:
+        up_x[i].wait_recv()
+        up_c.append(pass_on(up, q2, i, 1))
+    total = forward_part(fs * (chunks // 2) + part_size, part_size, total)
+    for _ in range(bits - 3):
+        pas_advance(0, 1, 2, 3)
+    for copy in up_c:
+        copy.wait_recv()
+    total = forward_part((1 - fs) * (chunks // 2), 2 * part_size, total)
     inv_rms = lax.rsqrt(jnp.sum(total, axis=1, keepdims=True) / width + norm_eps)
 
     pas_advance(0, 1, 2, 3)
@@ -325,7 +357,7 @@
         hit = jnp.where(col_at == pos_ref[fs * queries + q], 1.0, 0.0)
         onehot = onehot + jnp.where(row_at == q, hit, 0.0)
     term = jnp.log(jnp.broadcast_to(row_sum, (queries, pairs))) * (1.0 / pairs)
-    term = jnp.sum(term - 2.0 * scores * onehot)
+    term = jnp.sum(term - 2.0 * scores * onehot, axis=0, keepdims=True)
     at8 = lax.broadcasted_iota(jnp.int32, (8, pairs), 0)
     col_part = jnp.broadcast_to(jnp.sum(expo, axis=0, keepdims=True), (8, pairs))
     payload = jnp.where(at8 == 0, col_part, jnp.where(at8 == 1, term, 0.0))
@@ -335,14 +367,20 @@
     copies = [send(near.at[slot], near.at[slot], peer(m, f)) for m, f in near_masks]
 
     def own_side(j, totals):
+        totals, hidden_up = totals
         cols = cols_of(j)
         value = pooled[:, cols] * gain_ref[:, cols]
+        hidden_up = hidden_up + mm(hid[:, cols].astype(jnp.bfloat16), up[:, cols], nt)
         return tuple(
             totals[q] + fold(hid[of_query(q), cols] * value[q : q + 1]) for q in range(queries)
-        )
-
-    own = loop(
-        own_side, tuple(jnp.zeros((LEN, lanes), jnp.float32) for _ in range(queries))
+        ), hidden_up
+
+    own, hidden_up = loop(
+        own_side,
+        (
+            tuple(jnp.zeros((LEN, lanes), jnp.float32) for _ in range(queries)),
+            jnp.zeros((tokens, rank), jnp.float32),
+        ),
     )
     own = [
         jnp.sum(own[q], axis=1, keepdims=True) * inv_length[q : q + 1] for q in range(queries)
@@ -361,9 +399,6 @@
     for k in range(1, groups // 4):
         summed = summed + far[k]
     col_sum = summed[0:1]
-    loss_ref[0, 0] = (
-        jnp.sum(jnp.log(col_sum) + summed[1:2] * (1.0 / pairs)) / (2.0 * pairs) + inv_temp
-    )
     weights = 0.5 * (expo / row_sum + expo / col_sum) - onehot
     weights = weights.astype(jnp.bfloat16).astype(jnp.float32)
     along = jnp.sum(weights * scores, axis=1, keepdims=True)
@@ -378,20 +413,25 @@
     both = jnp.concatenate([high, weights - high], axis=0).astype(jnp.bfloat16)
     inward = inv_length * along
 
-    def hidden_side(j, total):
+    def query_side(j, total):
         cols = cols_of(j)
         two = mm(both, pasm[:, cols], nn)
-        scaled = two[:queries] + two[queries:] - pooled[:, cols] * inward
-        scaled = scaled * shrink * gain_ref[:, cols]
+        value = two[:queries] + two[queries:] - pooled[:, cols] * inward
+        value = value * shrink * gain_ref[:, cols]
+        scaled[:, cols] = value
+        return total + mm(value.astype(jnp.bfloat16), up[:, cols], nt)
+
+    def hidden_side(j, _):
+        cols = cols_of(j)
         value = jnp.concatenate(
             [
-                inv_rms[of_query(q)] * scaled[q : q + 1] - hid[of_query(q), cols] * back[q]
+                inv_rms[of_query(q)] * scaled[q : q + 1, cols] - hid[of_query(q), cols] * back[q]
                 for q in range(queries)
             ],
             axis=0,
         ).astype(jnp.bfloat16)
         put(1, j, adapter_scale_factor * mm(code_t, value, nn))
-        return total + mm(value, up[:, cols], nt)
+        return 0
 
     def put(g, j, grad):
         grad = grad.astype(jnp.bfloat16)
@@ -405,7 +445,20 @@
         return lax.fori_loop(0, chunks // 2, of, init, unroll=2)
 
     theirs, ours = 1 - bit[0], bit[0]
-    code_grad = sided(hidden_side, theirs, jnp.zeros((tokens, rank), jnp.float32))
+    query_up = loop(query_side, jnp.zeros((queries, rank), jnp.float32), 4)
+    code_grad = jnp.concatenate(
+        [
+            inv_rms[of_query(q)] * query_up[q : q + 1] - hidden_up[of_query(q)] * back[q]
+            for q in range(queries)
+        ],
+        axis=0,
+    )
+    code_grad_t = (adapter_scale_factor * code_grad).astype(jnp.bfloat16)
+    code_grad_t = code_grad_t.astype(jnp.float32).T.astype(jnp.bfloat16)
+
+    def input_side(j, _):
+        put(0, j, mm(code_grad_t, ain[:, cols_of(j)], nn))
+        return 0
 
     chains = grad_chains(bits)
     grad_copy = [None] * len(chains)
@@ -446,23 +499,26 @@
             else:
                 part[index] = value.astype(jnp.bfloat16)
 
-    early = [n for n, c in enumerate(chains) if c[0] == 1]
-    late = [n for n, c in enumerate(chains) if c[0] == 0]
+    early = [n for n, c in enumerate(chains) if c[0] == 0]
+    late = [n for n, c in enumerate(chains) if c[0] == 1]
+    sided(input_side, theirs, 0)
     for n in early:
         grad_send(n, 0)
-    code_grad = sided(hidden_side, ours, code_grad)
-    code_grad_t = (adapter_scale_factor * code_grad).astype(jnp.bfloat16)
-    code_grad_t = code_grad_t.astype(jnp.float32).T.astype(jnp.bfloat16)
-
-    def input_side(j, _):
-        put(0, j, mm(code_grad_t, ain[:, cols_of(j)], nn))
-        return 0
-
-    sided(input_side, theirs, 0)
+    sided(hidden_side, theirs, 0)
     for n in late:
         grad_send(n, 0)
     sided(input_side, ours, 0)
-    for k in range(steps):
+    for n in early:
+        grad_add(n, 0)
+        grad_send(n, 1)
+    sided(hidden_side, ours, 0)
+    for n in late:
+        grad_add(n, 0)
+        grad_send(n, 1)
+    loss_ref[0, 0] = (
+        jnp.sum(jnp.log(col_sum) + summed[1:2]) / (2.0 * pairs) + inv_temp
+    )
+    for k in range(1, steps):
         for n in early + late:
             grad_add(n, k)
             if k + 1 < steps:
@@ -502,7 +558,7 @@
     half = width // 2
     bf16, f32 = jnp.bfloat16, jnp.float32
     rx = grad_shapes(bits, rank, chunk)
-    copies = 80
+    copies = 96
     vmem = pl.BlockSpec(memory_space=pltpu.VMEM)
     smem = pl.BlockSpec(memory_space=pltpu.SMEM)
     hbm = pl.BlockSpec(memory_space=pl.ANY)
@@ -524,6 +580,7 @@
             pltpu.VMEM((pairs, width), bf16),
             pltpu.VMEM((2,) * bits + (2, 2, 2, rank // 4, chunk), bf16),
             pltpu.VMEM((queries, width), f32),
+            pltpu.VMEM((queries, width), f32),
             pltpu.VMEM((8, 8, pairs), f32),
             pltpu.VMEM((groups // 4, 8, pairs), f32),
             rx,

time: 65.6 us -> 64.1 us (0.977)
  Pallas kernels: 61.4 us -> 59.9 us
    pallas_call x1, Pallas kernels: 61.4 us -> 59.9 us  [fused_shards(): pl.pallas_call(functools.partial(fused, bits, (tokens, width, rank, queri...]
where the time goes in v4:
time: 64.1 us; the launch traced here: 63.9 us
  Pallas kernels  59.9 us (93%)
  between operations  2.45 us (4%)
  local copies, waits for them, and re-layouts  1.57 us (2%)
    pallas_call x1, Pallas kernels, fused_shards(): pl.pallas_call(functools.partial(fused, bits, (tokens, width, rank, queri...  59.9 us
    unnamed x1, local copies, waits for them, and re-layouts  1.57 us

profile of v4, /device:TPU:0, one launch (start us, length us, event | category | flops | bytes accessed | tf_op | source)
XLA Modules:
  0.0 63.9 jit_solution(11238399214332223087)
XLA Ops:
  0.6 59.9 %shard_map.86 = (f32[2,32,512]{2,1,0:T(8,128)}, f32[1,1]{1,0:T(1,128)}) custom-call(s32[8]{0:T(128)} %pos_ref.1, f32[1,8192]{1,0:T(1,128)} %bitcast.4, bf16[128,8192]{1,0:T(8,128)(2,1)} %ain_hbm.1, bf16[128,8192]{1,0:T(8,128)(2,1)} %frz_hbm.1, bf16[64,4096]{1,0:T(8,128)(2,1)} %bitcast.3, bf16[64,4096]{1,0:T(8,128)(2,1)} %up_hbm.1, bf16[8,4096]{1,0:T(8,128)(2,1)} %pas_hbm.1), custom_call_target="tpu_custom_call" | custom-call | tf_op jit(solution)/shard_map/pallas_call | solution.py:565
  60.5 1.6 %copy.11 = f32[2,32,512]{2,1,0:T(8,128)} copy(f32[2,32,512]{2,1,0:T(8,128)} %get-tuple-element.8) | data formatting | bytes 262144

commit v5 on v4

--- a/solution.py
+++ b/solution.py
@@ -182,7 +182,7 @@
     far_first = list(range(2, bits))[::-1]
     orders = (
         ["y", 1] + far_first + [0],
-        [1, "y"] + far_first + [0],
+        ["y", 1] + far_first + [0],
         far_first + [1, "y", 0],
         far_first + ["y", 1, 0],
     )
@@ -241,16 +241,18 @@
         at_y[i].wait_recv()
         at_x.append(pass_on(at, q0, i, 2))
         at_c.append(pass_on(at, q0, i, 1))
+    pas_advance(0, 1, 3)
     for i in pieces:
         up_y[i].wait_recv()
         up_x.append(pass_on(up, q0, i, 2))
         up_c.append(pass_on(up, q0, i, 1))
-    pas_advance(0, 1, 2, 3)
+    pas_advance(2)
     latent = latent + quarter_of(q0)
     for i in pieces:
         at_x[i].wait_recv()
         at_c.append(pass_on(at, q2, i, 1))
     latent = latent + quarter_of(q2)
+    pas_advance(0)
     for copy in at_c[:2]:
         copy.wait_recv()
     latent = latent + quarter_of(q1)
@@ -298,8 +300,7 @@
         up_x[i].wait_recv()
         up_c.append(pass_on(up, q2, i, 1))
     total = forward_part(fs * (chunks // 2) + part_size, part_size, total)
-    for _ in range(bits - 3):
-        pas_advance(0, 1, 2, 3)
+    pas_advance(1, 3, 2)
     for copy in up_c:
         copy.wait_recv()
     total = forward_part((1 - fs) * (chunks // 2), 2 * part_size, total)
@@ -608,7 +609,7 @@
     groups = mesh.shape["dp"]
     bits = groups.bit_length() - 1
     body = shards
-    if mesh.shape["fsdp"] == 2 and 8 <= groups <= 16 and groups == 2 ** bits:
+    if mesh.shape["fsdp"] == 2 and groups == 16:
         body = functools.partial(fused_shards, bits)
     return jax.shard_map(
         body, mesh=mesh, in_specs=placed, out_specs=(P(None, "fsdp", "dp"), P()), check_vma=False

time: 64.1 us -> 61.5 us (0.959)
  Pallas kernels: 59.9 us -> 57.2 us
    pallas_call x1, Pallas kernels: 59.9 us -> 57.2 us  [fused_shards(): pl.pallas_call(functools.partial(fused, bits, (tokens, width, rank, queri...]
where the time goes in v5:
time: 61.5 us; the launch traced here: 61.2 us
  Pallas kernels  57.2 us (93%)
  between operations  2.45 us (4%)
  local copies, waits for them, and re-layouts  1.57 us (3%)
    pallas_call x1, Pallas kernels, fused_shards(): pl.pallas_call(functools.partial(fused, bits, (tokens, width, rank, queri...  57.2 us
    unnamed x1, local copies, waits for them, and re-layouts  1.57 us

profile of v5, /device:TPU:0, one launch (start us, length us, event | category | flops | bytes accessed | tf_op | source)
XLA Modules:
  0.0 61.2 jit_solution(9112448353661662778)
XLA Ops:
  0.6 57.2 %shard_map.86 = (f32[2,32,512]{2,1,0:T(8,128)}, f32[1,1]{1,0:T(1,128)}) custom-call(s32[8]{0:T(128)} %pos_ref.1, f32[1,8192]{1,0:T(1,128)} %bitcast.4, bf16[128,8192]{1,0:T(8,128)(2,1)} %ain_hbm.1, bf16[128,8192]{1,0:T(8,128)(2,1)} %frz_hbm.1, bf16[64,4096]{1,0:T(8,128)(2,1)} %bitcast.3, bf16[64,4096]{1,0:T(8,128)(2,1)} %up_hbm.1, bf16[8,4096]{1,0:T(8,128)(2,1)} %pas_hbm.1), custom_call_target="tpu_custom_call" | custom-call | tf_op jit(solution)/shard_map/pallas_call | solution.py:566
  57.9 1.6 %copy.11 = f32[2,32,512]{2,1,0:T(8,128)} copy(f32[2,32,512]{2,1,0:T(8,128)} %get-tuple-element.8) | data formatting | bytes 262144

commit v6 on v5

--- a/solution.py
+++ b/solution.py
@@ -280,9 +280,14 @@
 
     def forward(j, total):
         cols = cols_of(j)
-        value = frz[:, cols].astype(jnp.float32) + adapter_scale_factor * mm(code, up[:, cols], nn)
-        hid[:, cols] = value
-        return total + fold(value * value)
+        added = mm(code, up[:, cols], nn)
+        sums = []
+        for at in range(0, tokens, LEN):
+            rows_at = slice(at, at + LEN)
+            value = frz[rows_at, cols].astype(jnp.float32) + adapter_scale_factor * added[rows_at]
+            hid[rows_at, cols] = value
+            sums.append(fold(value * value))
+        return total + jnp.concatenate(sums, axis=0)
 
     def loop(body, init, unroll=2):
         return lax.fori_loop(0, chunks, body, init, unroll=unroll)
@@ -462,39 +467,44 @@
         return 0
 
     chains = grad_chains(bits)
-    grad_copy = [None] * len(chains)
-    steps = bits + 1
-
-    def view(n, k, there):
+    grad_copies = [None] * len(chains)
+    steps = len(chains[0][2])
+    rx_of = iter(rx)
+    rx_at = [[[next(rx_of) for _ in hop_masks(hop)] for hop in order] for _, _, order in chains]
+
+    def view(n, k, mask):
         g, h, order = chains[n]
-        done, now = order[:k], order[k]
+        fixed = [axis for hop in order[: k + 1] for axis in hop]
+        flip = [axis for i, axis in enumerate(order[k]) if (mask >> i) & 1]
         index = ()
         for b in reversed(range(bits)):
-            if b == now:
-                index += (1 - bit[b] if there else bit[b],)
-            else:
-                index += (bit[b] if b in done else WHOLE,)
-        if now == "y":
-            return index + (g, 1 - fs if there else fs, h)
-        return index + (g, fs if "y" in done else WHOLE, h)
+            index += ((1 - bit[b] if b in flip else bit[b]) if b in fixed else WHOLE,)
+        y = (1 - fs if "y" in flip else fs) if "y" in fixed else WHOLE
+        return index + (g, y, h)
 
     def grad_send(n, k):
-        now = chains[n][2][k]
-        device = peer(0, 1) if now == "y" else peer(2 ** now, 0)
-        grad_copy[n] = send(part.at[view(n, k, True)], rx[n * steps + k], device)
+        hop = chains[n][2][k]
+        grad_copies[n] = []
+        for mask in hop_masks(hop):
+            flip = [axis for i, axis in enumerate(hop) if (mask >> i) & 1]
+            device = peer(sum(2 ** axis for axis in flip if axis != "y"), "y" in flip)
+            source = part.at[view(n, k, mask)]
+            grad_copies[n].append(send(source, rx_at[n][k][mask - 1], device))
 
     def grad_add(n, k):
         g, h, order = chains[n]
-        buffer = rx[n * steps + k]
-        kept = view(n, k, False)
-        grad_copy[n].wait_recv()
+        kept = view(n, k, 0)
+        for copy in grad_copies[n]:
+            copy.wait_recv()
         free = [at for at, i in enumerate(kept) if isinstance(i, slice)]
         for picks in itertools.product((0, 1), repeat=len(free)):
             index = list(kept)
             for at_dim, pick in zip(free, picks):
                 index[at_dim] = pick
             index = tuple(index)
-            value = part[index].astype(jnp.float32) + buffer[picks].astype(jnp.float32)
+            value = part[index].astype(jnp.float32)
+            for buffer in rx_at[n][k]:
+                value = value + buffer[picks].astype(jnp.float32)
             if k == len(order) - 1:
                 out_ref[g, h * rank // 4 : (h + 1) * rank // 4] = value
             else:
@@ -528,23 +538,27 @@
         copy.wait_send()
 
 
+def hop_masks(hop):
+    return range(1, 2 ** len(hop))
+
+
 def grad_chains(bits):
-    last = list(range(3, bits))
+    last = tuple(range(2, bits))
     return [
-        (1, 0, [0, 1, "y", 2] + last),
-        (1, 1, [0, 2, "y", 1] + last),
-        (0, 0, [0, "y", 1, 2] + last),
-        (0, 1, [0, 2, 1, "y"] + last),
+        (1, 0, [(0,), (1,), ("y",), last]),
+        (1, 1, [(0,), (2,), (1, "y"), last[1:]]),
+        (0, 0, [(0,), ("y",), (1,), last]),
+        (0, 1, [(0,), (2,), (1, "y"), last[1:]]),
     ]
 
 
 def grad_shapes(bits, rank, chunk):
     shapes = []
     for _, _, order in grad_chains(bits):
-        for k in range(len(order)):
-            gone = order[: k + 1]
-            free = bits - len([b for b in gone if b != "y"]) + (0 if "y" in gone else 1)
-            shapes.append(pltpu.VMEM((2,) * free + (rank // 4, chunk), jnp.bfloat16))
+        for k, hop in enumerate(order):
+            fixed = sum(len(each) for each in order[: k + 1])
+            shape = (2,) * (bits + 1 - fixed) + (rank // 4, chunk)
+            shapes += [pltpu.VMEM(shape, jnp.bfloat16) for _ in hop_masks(hop)]
     return shapes
 
 

time: 61.5 us -> 58.9 us (0.958)
  Pallas kernels: 57.2 us -> 54.7 us
    pallas_call x1, Pallas kernels: 57.2 us -> 54.7 us  [fused_shards(): pl.pallas_call(functools.partial(fused, bits, (tokens, width, rank, queri...]
where the time goes in v6:
time: 58.9 us; the launch traced here: 58.7 us
  Pallas kernels  54.7 us (93%)
  between operations  2.45 us (4%)
  local copies, waits for them, and re-layouts  1.57 us (3%)
    pallas_call x1, Pallas kernels, fused_shards(): pl.pallas_call(functools.partial(fused, bits, (tokens, width, rank, queri...  54.7 us
    unnamed x1, local copies, waits for them, and re-layouts  1.57 us

profile of v6, /device:TPU:0, one launch (start us, length us, event | category | flops | bytes accessed | tf_op | source)
XLA Modules:
  0.0 58.7 jit_solution(17786838286948049828)
XLA Ops:
  0.6 54.7 %shard_map.86 = (f32[2,32,512]{2,1,0:T(8,128)}, f32[1,1]{1,0:T(1,128)}) custom-call(s32[8]{0:T(128)} %pos_ref.1, f32[1,8192]{1,0:T(1,128)} %bitcast.4, bf16[128,8192]{1,0:T(8,128)(2,1)} %ain_hbm.1, bf16[128,8192]{1,0:T(8,128)(2,1)} %frz_hbm.1, bf16[64,4096]{1,0:T(8,128)(2,1)} %bitcast.3, bf16[64,4096]{1,0:T(8,128)(2,1)} %up_hbm.1, bf16[8,4096]{1,0:T(8,128)(2,1)} %pas_hbm.1), custom_call_target="tpu_custom_call" | custom-call | tf_op jit(solution)/shard_map/pallas_call | solution.py:580
  55.3 1.6 %copy.11 = f32[2,32,512]{2,1,0:T(8,128)} copy(f32[2,32,512]{2,1,0:T(8,128)} %get-tuple-element.8) | data formatting | bytes 262144

commit v7 on v6

--- a/solution.py
+++ b/solution.py
@@ -179,12 +179,13 @@
         view = whole.at[:, q_at(q, other, i)]
         return send(view, view, peer(mask, 0))
 
-    far_first = list(range(2, bits))[::-1]
+    far_first = tuple(range(2, bits))[::-1]
+    apart = [(b,) for b in far_first]
     orders = (
-        ["y", 1] + far_first + [0],
-        ["y", 1] + far_first + [0],
-        far_first + [1, "y", 0],
-        far_first + ["y", 1, 0],
+        [("y", 1)] + apart + [(0,)],
+        [("y", 1)] + apart + [(0,)],
+        [far_first, (1,), ("y",), (0,)],
+        [far_first, ("y",), (1,), (0,)],
     )
     strips = len(orders)
     strip = half // strips
@@ -196,31 +197,30 @@
             if pas_copy[s] is not None:
                 for copy in pas_copy[s]:
                     copy.wait_recv()
-            done = orders[s][: pas_step[s]]
+            hops = orders[s][: pas_step[s]]
             pas_step[s] += 1
-            if len(done) == len(orders[s]):
+            if len(hops) == len(orders[s]):
                 continue
-            now = orders[s][len(done)]
+            done = [axis for hop in hops for axis in hop]
+            hop = orders[s][len(hops)]
             index = tuple(WHOLE if b in done else bit[b] for b in reversed(range(bits)))
-            device = peer(0, 1) if now == "y" else peer(2 ** now, 0)
             place = pl.multiple_of(fs * half + s * strip, strip)
-            if not done:
-                source = pas_hbm.at[:, s * strip : (s + 1) * strip]
-                target = pas.at[index + (WHOLE, pl.ds(place, strip))]
-                pas_copy[s] = [send(source, target, device)]
-                continue
-            places = [place]
-            if "y" in done:
-                places = [h * half + s * strip for h in (0, 1)]
-            views = [pas.at[index + (WHOLE, pl.ds(p, strip))] for p in places]
-            pas_copy[s] = [send(v, v, device) for v in views]
+            places = [h * half + s * strip for h in (0, 1)] if "y" in done else [place]
+            pas_copy[s] = []
+            for mask in hop_masks(hop):
+                flip = [axis for i, axis in enumerate(hop) if (mask >> i) & 1]
+                device = peer(sum(2 ** axis for axis in flip if axis != "y"), "y" in flip)
+                for p in places:
+                    target = pas.at[index + (WHOLE, pl.ds(p, strip))]
+                    source = target if done else pas_hbm.at[:, s * strip : (s + 1) * strip]
+                    pas_copy[s].append(send(source, target, device))
 
     pas_advance(0, 1, 2, 3)
     at_y = across(at, at_hbm)
     up_y = across(up, up_hbm)
 
     loads[2].wait()
-    pas_advance(0, 1, 2, 3)
+    pas_advance(0, 1)
 
     nn = (((1,), (0,)), ((), ()))
     nt = (((1,), (1,)), ((), ()))
@@ -241,18 +241,18 @@
         at_y[i].wait_recv()
         at_x.append(pass_on(at, q0, i, 2))
         at_c.append(pass_on(at, q0, i, 1))
-    pas_advance(0, 1, 3)
+    pas_advance(3)
     for i in pieces:
         up_y[i].wait_recv()
         up_x.append(pass_on(up, q0, i, 2))
         up_c.append(pass_on(up, q0, i, 1))
-    pas_advance(2)
+    pas_advance(2, 0)
     latent = latent + quarter_of(q0)
     for i in pieces:
         at_x[i].wait_recv()
         at_c.append(pass_on(at, q2, i, 1))
     latent = latent + quarter_of(q2)
-    pas_advance(0)
+    pas_advance(1)
     for copy in at_c[:2]:
         copy.wait_recv()
     latent = latent + quarter_of(q1)
@@ -305,7 +305,7 @@
         up_x[i].wait_recv()
         up_c.append(pass_on(up, q2, i, 1))
     total = forward_part(fs * (chunks // 2) + part_size, part_size, total)
-    pas_advance(1, 3, 2)
+    pas_advance(3, 2)
     for copy in up_c:
         copy.wait_recv()
     total = forward_part((1 - fs) * (chunks // 2), 2 * part_size, total)

time: 58.9 us -> 59.4 us (level)
  no operation moved by 1% of the time
where the time goes in v7:
time: 59.4 us; the launch traced here: 59.1 us
  Pallas kernels  55.1 us (93%)
  between operations  2.45 us (4%)
  local copies, waits for them, and re-layouts  1.57 us (3%)
    pallas_call x1, Pallas kernels, fused_shards(): pl.pallas_call(functools.partial(fused, bits, (tokens, width, rank, queri...  55.1 us
    unnamed x1, local copies, waits for them, and re-layouts  1.57 us

profile of v7, /device:TPU:0, one launch (start us, length us, event | category | flops | bytes accessed | tf_op | source)
XLA Modules:
  0.0 59.1 jit_solution(3359784034740927596)
XLA Ops:
  0.6 55.1 %shard_map.86 = (f32[2,32,512]{2,1,0:T(8,128)}, f32[1,1]{1,0:T(1,128)}) custom-call(s32[8]{0:T(128)} %pos_ref.1, f32[1,8192]{1,0:T(1,128)} %bitcast.4, bf16[128,8192]{1,0:T(8,128)(2,1)} %ain_hbm.1, bf16[128,8192]{1,0:T(8,128)(2,1)} %frz_hbm.1, bf16[64,4096]{1,0:T(8,128)(2,1)} %bitcast.3, bf16[64,4096]{1,0:T(8,128)(2,1)} %up_hbm.1, bf16[8,4096]{1,0:T(8,128)(2,1)} %pas_hbm.1), custom_call_target="tpu_custom_call" | custom-call | tf_op jit(solution)/shard_map/pallas_call | solution.py:580
  55.8 1.6 %copy.11 = f32[2,32,512]{2,1,0:T(8,128)} copy(f32[2,32,512]{2,1,0:T(8,128)} %get-tuple-element.8) | data formatting | bytes 262144

commit v8 on v7

--- a/solution.py
+++ b/solution.py
@@ -184,8 +184,8 @@
     orders = (
         [("y", 1)] + apart + [(0,)],
         [("y", 1)] + apart + [(0,)],
-        [far_first, (1,), ("y",), (0,)],
-        [far_first, ("y",), (1,), (0,)],
+        apart + [(1,), ("y",), (0,)],
+        apart + [("y",), (1,), (0,)],
     )
     strips = len(orders)
     strip = half // strips
@@ -220,7 +220,7 @@
     up_y = across(up, up_hbm)
 
     loads[2].wait()
-    pas_advance(0, 1)
+    pas_advance(0, 1, 2, 3)
 
     nn = (((1,), (0,)), ((), ()))
     nt = (((1,), (1,)), ((), ()))

time: 59.4 us -> 59.4 us (level)
  no operation moved by 1% of the time
where the time goes in v8:
time: 59.4 us; the launch traced here: 59.1 us
  Pallas kernels  55.1 us (93%)
  between operations  2.45 us (4%)
  local copies, waits for them, and re-layouts  1.57 us (3%)
    pallas_call x1, Pallas kernels, fused_shards(): pl.pallas_call(functools.partial(fused, bits, (tokens, width, rank, queri...  55.1 us
    unnamed x1, local copies, waits for them, and re-layouts  1.57 us

profile of v8, /device:TPU:0, one launch (start us, length us, event | category | flops | bytes accessed | tf_op | source)
XLA Modules:
  0.0 59.1 jit_solution(3153311412441874217)
XLA Ops:
  0.6 55.1 %shard_map.86 = (f32[2,32,512]{2,1,0:T(8,128)}, f32[1,1]{1,0:T(1,128)}) custom-call(s32[8]{0:T(128)} %pos_ref.1, f32[1,8192]{1,0:T(1,128)} %bitcast.4, bf16[128,8192]{1,0:T(8,128)(2,1)} %ain_hbm.1, bf16[128,8192]{1,0:T(8,128)(2,1)} %frz_hbm.1, bf16[64,4096]{1,0:T(8,128)(2,1)} %bitcast.3, bf16[64,4096]{1,0:T(8,128)(2,1)} %up_hbm.1, bf16[8,4096]{1,0:T(8,128)(2,1)} %pas_hbm.1), custom_call_target="tpu_custom_call" | custom-call | tf_op jit(solution)/shard_map/pallas_call | solution.py:580
  55.8 1.6 %copy.11 = f32[2,32,512]{2,1,0:T(8,128)} copy(f32[2,32,512]{2,1,0:T(8,128)} %get-tuple-element.8) | data formatting | bytes 262144
